TPU v7x, 32 devices: a whole 2x2x4 slice. The times are simulated.
32 devices in a mesh: blk: 8 (over y, x, core), grp: 4 (over z).
Axes of the slice: x: 2, y: 2, z: 4, core: 2. Of those that a mesh axis runs over, the one named last changes fastest.
Arguments:
- images: bfloat16 [64, 3, 1024], P(('blk', 'grp')), may hold values from -10 to 10
Outputs:
- kernel_window: float32 [64, 5, 8], P(('blk', 'grp'))
All inputs are finite; a program needn't handle non-finite values.
Results may differ from a plain program's by a relative error of at most 0.0003.
Values may be sent and summed in bfloat16 or wider, within the bound.
A program may use at most 64 MiB of HBM per device.

v0:
```python
import jax
import jax.numpy as jnp
from jax import lax
from jax.sharding import PartitionSpec as P

SIDE = 32
LAYERS = 3
ROUNDS = 2


bias_var = 0.1


def shifted(block, axis, distance):
    devices = range(lax.axis_size(axis))
    route = [((i - distance) % len(devices), i) for i in devices]
    return lax.ppermute(block, axis, route)


def stencil_band(side):
    positions = jnp.arange(side)
    return (jnp.abs(positions[:, None] - positions[None, :]) <= 1).astype(jnp.float32)


def stencil_maps(pair_maps, band_matrix):
    shaped = pair_maps.reshape(pair_maps.shape[:-1] + (SIDE, SIDE))
    first = jnp.einsum("ab,...bc->...ac", band_matrix, shaped, precision=lax.Precision.HIGHEST)
    second = jnp.einsum("...ac,dc->...ad", first, band_matrix, precision=lax.Precision.HIGHEST)
    return (second / 9.0).reshape(pair_maps.shape)


def variance_maps(image_data, band_matrix):
    current = stencil_maps(jnp.mean(image_data * image_data, axis=1), band_matrix) + bias_var
    layers_out = [current]
    for layer in range(LAYERS - 1):
        current = stencil_maps(current, band_matrix) + bias_var
        layers_out.append(current)
    return jnp.stack(layers_out, 0)


def relu_expect(cov_map, var_left, var_right):
    scale_root = jnp.sqrt(var_left * var_right)
    ratio = jnp.clip(cov_map / scale_root, -1.0, 1.0)
    angle_map = jnp.arccos(ratio)
    return (
        scale_root * (jnp.sqrt(1.0 - ratio * ratio) + (jnp.pi - angle_map) * ratio) / (2.0 * jnp.pi)
    )


def pair_kernel(left_img, right_img, left_var, right_var, band_matrix):
    product = (
        jnp.einsum("acp,bcp->abp", left_img, right_img, preferred_element_type=jnp.float32)
        / left_img.shape[1]
    )
    cov_map = stencil_maps(product, band_matrix) + bias_var
    expect = cov_map
    for layer in range(LAYERS):
        expect = relu_expect(cov_map, left_var[layer][:, None, :], right_var[layer][None, :, :])
        if layer < LAYERS - 1:
            cov_map = 2.0 * stencil_maps(expect, band_matrix) + bias_var
    return jnp.mean(2.0 * expect, axis=-1)


def per_device(images):
    band_matrix = stencil_band(SIDE)
    own_var = variance_maps(images.astype(jnp.float32), band_matrix)
    whole_block = lax.all_gather(images, "grp", axis=0, tiled=True)
    kernel_tiles = {
        0: pair_kernel(
            images,
            whole_block,
            own_var,
            variance_maps(whole_block.astype(jnp.float32), band_matrix),
            band_matrix,
        )
    }
    visitor_block = whole_block
    for step_index in range(1, ROUNDS + 1):
        visitor_block = shifted(visitor_block, "blk", 1)
        kernel_tiles[-step_index] = pair_kernel(
            images,
            visitor_block,
            own_var,
            variance_maps(visitor_block.astype(jnp.float32), band_matrix),
            band_matrix,
        )
    for step_index in range(1, ROUNDS + 1):
        mirrored = shifted(kernel_tiles[-step_index], "blk", -step_index)
        turned = lax.all_to_all(mirrored, "grp", split_axis=1, concat_axis=0, tiled=True)
        kernel_tiles[step_index] = jnp.transpose(turned)
    return jnp.stack([kernel_tiles[offset] for offset in range(-ROUNDS, ROUNDS + 1)], 1)


def solution(mesh):
    in_specs = (P(("blk", "grp"), None, None),)
    out_specs = P(("blk", "grp"), None, None)
    return jax.shard_map(
        per_device, mesh=mesh, in_specs=in_specs, out_specs=out_specs, check_vma=False
    )
```

profile of v0, /device:TPU:0, one launch (start us, length us, event | category | flops | bytes accessed | tf_op | source)
XLA Modules:
  0.0 77.9 jit_solution(6717188289155102285)
XLA Ops:
  0.0 0.7 copy.135
  0.7 14.9 %all_gather.3 = bf16[8,3,1024]{2,1,0:T(4,128)(2,1)S(1)} all-gather(bf16[2,3,1024]{2,1,0:T(4,128)(2,1)S(1)} %copy.135), channel_id=1, replica_groups=mesh['blk'=8,'grp'=4] {'grp'}, dimensions={0}, use_global_device_ids=true | all-gather | bytes 61440 | tf_op jit(solution)/shard_map/all_gather | solution.py:67
  15.7 1.8 %copy.145 = bf16[2,3,1024]{1,0,2:T(2,128)(2,1)} copy(bf16[2,3,1024]{2,0,1:T(2,128)(2,1)} %param.1) | data formatting | bytes 24576 | tf_op args[0]
  17.5 0.7 multiply_reduce_fusion.6
  18.3 1.5 %copy.175 = bf16[8,3,1024]{1,0,2:T(8,128)(2,1)S(1)} copy(bf16[8,3,1024]{2,1,0:T(4,128)(2,1)S(1)} %all_gather.3) | data formatting | bytes 98304 | tf_op jit(solution)/shard_map/all_gather | solution.py:67
  21.0 2.3 %convolution_multiply_fusion.2 = f32[1024,8,2]{1,2,0:T(2,128)S(1)} fusion(bf16[8,3,1024]{1,0,2:T(8,128)(2,1)S(1)} %copy.175, bf16[2,3,1024]{1,0,2:T(2,128)(2,1)} %copy.145), kind=kOutput, calls=%fused_computation.2 | convolution fusion | flops 114688 | bytes 126976 | tf_op jit(solution)/shard_map/acp,bcp->abp/dot_general | solution.py:52
  23.2 0.7 copy.177
  24.5 0.4 copy.169
  25.0 0.3 fusion.33
  25.6 0.4 fusion.24
  26.1 1.0 %convolution_bitcast_fusion.1 = f32[2,8,32,32]{2,3,1,0:T(8,128)S(1)} fusion(f32[2,8,32,32]{3,2,1,0:T(8,128)S(1)} %fusion.24, f32[8,32,32]{2,1,0:T(8,128)S(1)} %fusion.33, f32[2,32,32]{2,1,0:T(8,128)S(1)} %fusion.38), kind=kOutput, calls=%fused_computation.31 | convolution fusion | flops 6474752 | bytes 172032 | tf_op jit(solution)/shard_map/ab,...bc->...ac/dot_general | solution.py:27
  27.1 0.3 fusion.34
  27.7 0.4 fusion.25
  28.1 1.7 %convolution_bitcast_fusion = f32[2,8,32,32]{2,3,1,0:T(8,128)} fusion(f32[2,8,32,32]{3,2,1,0:T(8,128)S(1)} %fusion.25, f32[8,32,32]{2,1,0:T(8,128)S(1)} %fusion.34, f32[2,32,32]{2,1,0:T(8,128)S(1)} %fusion.37), kind=kOutput, calls=%fused_computation.30 | convolution fusion | flops 6474752 | bytes 172032 | tf_op jit(solution)/shard_map/ab,...bc->...ac/dot_general | solution.py:27
  30.4 0.7 copy.159
  31.1 1.2 %convolution_multiply_fusion = f32[1024,8,2]{1,2,0:T(2,128)S(1)} fusion(bf16[8,3,1024]{0,1,2:T(4,128)(2,1)S(1)} %copy.159, bf16[2,3,1024]{1,0,2:T(2,128)(2,1)S(1)} %copy-done), kind=kOutput, calls=%fused_computation | convolution fusion | flops 114688 | bytes 126976 | tf_op jit(solution)/shard_map/acp,bcp->abp/dot_general | solution.py:52
  32.3 0.9 %copy.161 = f32[2,8,32,32]{2,3,1,0:T(8,128)S(1)} copy(f32[2,8,32,32]{1,0,3,2:T(2,128)S(1)} %bitcast.209) | data formatting | bytes 131072 | tf_op jit(solution)/shard_map/reshape | solution.py:26
  33.7 0.4 copy.153
  34.3 0.3 fusion.30
  34.9 0.4 fusion.21
  35.3 1.0 %convolution_bitcast_fusion.4 = f32[2,8,32,32]{2,3,1,0:T(8,128)S(1)} fusion(f32[2,8,32,32]{3,2,1,0:T(8,128)S(1)} %fusion.21, f32[8,32,32]{2,1,0:T(8,128)S(1)} %fusion.30, f32[2,32,32]{2,1,0:T(8,128)S(1)} %fusion.38), kind=kOutput, calls=%fused_computation.34 | convolution fusion | flops 6474752 | bytes 172032 | tf_op jit(solution)/shard_map/ab,...bc->...ac/dot_general | solution.py:27
  36.4 0.3 fusion.31
  37.0 0.4 fusion.22
  37.4 1.0 %convolution_bitcast_fusion.3 = f32[2,8,32,32]{2,3,1,0:T(8,128)S(1)} fusion(f32[2,8,32,32]{3,2,1,0:T(8,128)S(1)} %fusion.22, f32[8,32,32]{2,1,0:T(8,128)S(1)} %fusion.31, f32[2,32,32]{2,1,0:T(8,128)S(1)} %fusion.37), kind=kOutput, calls=%fused_computation.33 | convolution fusion | flops 6474752 | bytes 172032 | tf_op jit(solution)/shard_map/ab,...bc->...ac/dot_general | solution.py:27
  38.4 0.3 fusion.32
  38.7 1.1 %multiply_reduce_fusion.1 = f32[2,8]{1,0:T(2,128)S(1)} fusion(f32[2,8,32,32]{2,3,1,0:T(8,128)S(1)} %convolution_bitcast_fusion.3, f32[8,32,32]{2,1,0:T(8,128)S(1)} %fusion.32, f32[2,32,32]{2,1,0:T(8,128)S(1)} %fusion.36), kind=kOutput, calls=%fused_computation.113 | convolution fusion | flops 6556656 | bytes 106560 | tf_op jit(solution)/shard_map/...ac,dc->...ad/dot_general | solution.py:28
  39.9 2.6 %collective-permute-start.2 = (f32[2,8]{1,0:T(2,128)S(1)}, f32[2,8]{1,0:T(2,128)S(1)}, u32[]{:S(2)}, u32[]{:S(2)}) collective-permute-start(f32[2,8]{1,0:T(2,128)S(1)} %broadcast_multiply_fusion.4), channel_id=1, source_target_pairs={{4,0},{8,4},{12,8},{16,12},{20,16},{24,20},{28,24},{0,28},{5,1},{9... | collective-permute-start | bytes 200 | tf_op jit(solution)/shard_map/ppermute | solution.py:17
  42.5 1.3 %collective-permute-done.2 = f32[2,8]{1,0:T(2,128)S(1)} collective-permute-done((f32[2,8]{1,0:T(2,128)S(1)}, f32[2,8]{1,0:T(2,128)S(1)}, u32[]{:S(2)}, u32[]{:S(2)}) %collective-permute-start.2) | collective-permute-done | bytes 96 | tf_op jit(solution)/shard_map/ppermute | solution.py:17
  43.9 0.6 copy.183
  44.5 4.7 %all-to-all-start = ((f32[2,4,2]{2,0,1:T(2,128)}), f32[2,4,2]{2,0,1:T(2,128)S(1)}, u32[]{:S(2)}, u32[]{:S(2)}) async-start(f32[2,4,2]{2,0,1:T(2,128)} %copy.183), calls=%async_computation | async-start | bytes 8192 | tf_op jit(solution)/shard_map/all_to_all | solution.py:89
  49.2 1.1 %multiply_reduce_fusion = f32[2,8]{1,0:T(2,128)S(1)} fusion(f32[2,8,32,32]{2,3,1,0:T(8,128)S(1)} %copy-done.2, f32[8,32,32]{2,1,0:T(8,128)S(1)} %fusion.35, f32[2,32,32]{2,1,0:T(8,128)S(1)} %fusion.36), kind=kOutput, calls=%fused_computation.84 | convolution fusion | flops 6556656 | bytes 106560 | tf_op jit(solution)/shard_map/...ac,dc->...ad/dot_general | solution.py:28
  50.4 4.5 %all-to-all-done = f32[2,4,2]{2,0,1:T(2,128)S(1)} async-done(((f32[2,4,2]{2,0,1:T(2,128)}), f32[2,4,2]{2,0,1:T(2,128)S(1)}, u32[]{:S(2)}, u32[]{:S(2)}) %all-to-all-start) | async-done | bytes 96 | tf_op jit(solution)/shard_map/all_to_all | solution.py:89
  54.9 0.7 copy.144
  55.6 1.2 %convolution_multiply_fusion.1 = f32[1024,8,2]{1,2,0:T(2,128)S(1)} fusion(bf16[8,3,1024]{0,1,2:T(4,128)(2,1)S(1)} %copy.144, bf16[2,3,1024]{1,0,2:T(2,128)(2,1)S(1)} %copy-done), kind=kOutput, calls=%fused_computation.1 | convolution fusion | flops 114688 | bytes 126976 | tf_op jit(solution)/shard_map/acp,bcp->abp/dot_general | solution.py:52
  56.8 0.7 copy.146
  58.0 0.4 copy.138
  58.6 0.3 fusion.27
  59.2 0.4 fusion.18
  59.6 1.0 %convolution_bitcast_fusion.7 = f32[2,8,32,32]{2,3,1,0:T(8,128)S(1)} fusion(f32[2,8,32,32]{3,2,1,0:T(8,128)S(1)} %fusion.18, f32[8,32,32]{2,1,0:T(8,128)S(1)} %fusion.27, f32[2,32,32]{2,1,0:T(8,128)S(1)} %fusion.38), kind=kOutput, calls=%fused_computation.37 | convolution fusion | flops 6474752 | bytes 172032 | tf_op jit(solution)/shard_map/ab,...bc->...ac/dot_general | solution.py:27
  61.3 0.4 fusion.19
  61.7 1.0 %convolution_bitcast_fusion.6 = f32[2,8,32,32]{2,3,1,0:T(8,128)S(1)} fusion(f32[2,8,32,32]{3,2,1,0:T(8,128)S(1)} %fusion.19, f32[8,32,32]{2,1,0:T(8,128)S(1)} %fusion.28, f32[2,32,32]{2,1,0:T(8,128)S(1)} %fusion.37), kind=kOutput, calls=%fused_computation.36 | convolution fusion | flops 6474752 | bytes 172032 | tf_op jit(solution)/shard_map/ab,...bc->...ac/dot_general | solution.py:27
  63.0 1.1 %multiply_reduce_fusion.2 = f32[2,8]{1,0:T(2,128)S(1)} fusion(f32[2,8,32,32]{2,3,1,0:T(8,128)S(1)} %convolution_bitcast_fusion.6, f32[8,32,32]{2,1,0:T(8,128)S(1)} %fusion.29, f32[2,32,32]{2,1,0:T(8,128)S(1)} %fusion.36), kind=kOutput, calls=%fused_computation.142 | convolution fusion | flops 6556656 | bytes 106560 | tf_op jit(solution)/shard_map/...ac,dc->...ad/dot_general | solution.py:28
  64.2 1.6 %collective-permute-start.3 = (f32[2,8]{1,0:T(2,128)S(1)}, f32[2,8]{1,0:T(2,128)S(1)}, u32[]{:S(2)}, u32[]{:S(2)}) collective-permute-start(f32[2,8]{1,0:T(2,128)S(1)} %broadcast_multiply_fusion.5), channel_id=1, source_target_pairs={{8,0},{12,4},{16,8},{20,12},{24,16},{28,20},{0,24},{4,28},{9,1},{1... | collective-permute-start | bytes 200 | tf_op jit(solution)/shard_map/ppermute | solution.py:17
  65.8 2.0 %collective-permute-done.3 = f32[2,8]{1,0:T(2,128)S(1)} collective-permute-done((f32[2,8]{1,0:T(2,128)S(1)}, f32[2,8]{1,0:T(2,128)S(1)}, u32[]{:S(2)}, u32[]{:S(2)}) %collective-permute-start.3) | collective-permute-done | bytes 96 | tf_op jit(solution)/shard_map/ppermute | solution.py:17
  67.9 0.6 copy.185
  68.5 3.2 %all-to-all-start.1 = ((f32[2,4,2]{2,0,1:T(2,128)}), f32[2,4,2]{2,0,1:T(2,128)S(1)}, u32[]{:S(2)}, u32[]{:S(2)}) async-start(f32[2,4,2]{2,0,1:T(2,128)} %copy.185), calls=%async_computation.1 | async-start | bytes 8192 | tf_op jit(solution)/shard_map/all_to_all | solution.py:89
  71.8 5.5 %all-to-all-done.1 = f32[2,4,2]{2,0,1:T(2,128)S(1)} async-done(((f32[2,4,2]{2,0,1:T(2,128)}), f32[2,4,2]{2,0,1:T(2,128)S(1)}, u32[]{:S(2)}, u32[]{:S(2)}) %all-to-all-start.1) | async-done | bytes 96 | tf_op jit(solution)/shard_map/all_to_all | solution.py:89
  77.4 0.6 constant_dynamic-update-slice_fusion
  (52 shorter events, 6.6 us)
Async XLA Ops:
  15.6 14.7 %collective-permute-start = (bf16[8,3,1024]{2,0,1:T(8,128)(2,1)S(1)}, bf16[8,3,1024]{2,0,1:T(8,128)(2,1)S(1)}, u32[]{:S(2)}, u32[]{:S(2)}) collective-permute-start(bf16[8,3,1024]{2,0,1:T(8,128)(2,1)S(1)} %get-tuple-element.6), channel_id=1, source_target_pairs={{28,0},{0,4},{4,8},{8,12},{12,16},{16,20},{20,24},{24,28},{29,1},{... | collective-permute-start | bytes 147464 | tf_op jit(solution)/shard_map/ppermute | solution.py:17
  27.1 4.0 %copy-start = (bf16[2,3,1024]{1,0,2:T(2,128)(2,1)S(1)}, bf16[2,3,1024]{1,0,2:T(2,128)(2,1)}, u32[]{:S(2)}) copy-start(bf16[2,3,1024]{1,0,2:T(2,128)(2,1)} %copy.145) | copy-start | bytes 36868
  37.0 12.3 %copy-start.2 = (f32[2,8,32,32]{2,3,1,0:T(8,128)S(1)}, f32[2,8,32,32]{2,3,1,0:T(8,128)}, u32[]{:S(2)}) copy-start(f32[2,8,32,32]{2,3,1,0:T(8,128)} %convolution_bitcast_fusion) | copy-start | bytes 196612
  39.9 3.9 %collective-permute-start.2 = (f32[2,8]{1,0:T(2,128)S(1)}, f32[2,8]{1,0:T(2,128)S(1)}, u32[]{:S(2)}, u32[]{:S(2)}) collective-permute-start(f32[2,8]{1,0:T(2,128)S(1)} %broadcast_multiply_fusion.4), channel_id=1, source_target_pairs={{4,0},{8,4},{12,8},{16,12},{20,16},{24,20},{28,24},{0,28},{5,1},{9... | collective-permute-start | bytes 200 | tf_op jit(solution)/shard_map/ppermute | solution.py:17
  42.5 12.4 %collective-permute-start.1 = (bf16[8,3,1024]{2,0,1:T(8,128)(2,1)S(1)}, bf16[8,3,1024]{2,0,1:T(8,128)(2,1)S(1)}, u32[]{:S(2)}, u32[]{:S(2)}) collective-permute-start(bf16[8,3,1024]{2,0,1:T(8,128)(2,1)S(1)} %collective-permute-done), channel_id=1, source_target_pairs={{28,0},{0,4},{4,8},{8,12},{12,16},{16,20},{20,24},{24,28},{29,1},{... | collective-permute-start | bytes 147464 | tf_op jit(solution)/shard_map/ppermute | solution.py:17
  44.5 10.3 %all-to-all-start = ((f32[2,4,2]{2,0,1:T(2,128)}), f32[2,4,2]{2,0,1:T(2,128)S(1)}, u32[]{:S(2)}, u32[]{:S(2)}) async-start(f32[2,4,2]{2,0,1:T(2,128)} %copy.183), calls=%async_computation | async-start | bytes 8192 | tf_op jit(solution)/shard_map/all_to_all | solution.py:89
  64.2 3.6 %collective-permute-start.3 = (f32[2,8]{1,0:T(2,128)S(1)}, f32[2,8]{1,0:T(2,128)S(1)}, u32[]{:S(2)}, u32[]{:S(2)}) collective-permute-start(f32[2,8]{1,0:T(2,128)S(1)} %broadcast_multiply_fusion.5), channel_id=1, source_target_pairs={{8,0},{12,4},{16,8},{20,12},{24,16},{28,20},{0,24},{4,28},{9,1},{1... | collective-permute-start | bytes 200 | tf_op jit(solution)/shard_map/ppermute | solution.py:17
  68.5 8.8 %all-to-all-start.1 = ((f32[2,4,2]{2,0,1:T(2,128)}), f32[2,4,2]{2,0,1:T(2,128)S(1)}, u32[]{:S(2)}, u32[]{:S(2)}) async-start(f32[2,4,2]{2,0,1:T(2,128)} %copy.185), calls=%async_computation.1 | async-start | bytes 8192 | tf_op jit(solution)/shard_map/all_to_all | solution.py:89
  71.7 5.6 %copy-start.1 = (f32[2,5,8]{2,0,1:T(2,128)}, f32[2,5,8]{2,0,1:T(2,128)S(1)}, u32[]{:S(2)}) copy-start(f32[2,5,8]{2,0,1:T(2,128)S(1)} %constant_dynamic-update-slice_fusion.1) | copy-start | bytes 964
where the time goes:
time: 78.3 us; the launch traced here: 77.9 us
  matrix products  24.5 us (31%)
  blocking collectives  14.9 us (19%)
  waiting for transfers between devices  13.3 us (17%)
  starting transfers between devices  12.3 us (16%)
  local copies, waits for them, and re-layouts  11.5 us (15%)
  other arithmetic  0.97 us (1%)
    all_gather x1, blocking collectives, per_device(): whole_block = lax.all_gather(images, 'grp', axis=0, tiled=True)  14.9 us
    dot_general x21, matrix products, stencil_maps(): jnp.einsum('ab,...bc->...ac', band_matrix, shaped, precision=lax.Precisio...  10.7 us
    all_to_all x2, waiting for transfers between devices, per_device(): lax.all_to_all(mirrored, 'grp', split_axis=1, concat_axis=0, tiled=True)  9.97 us
    dot_general x21, matrix products, stencil_maps(): jnp.einsum('...ac,dc->...ad', first, band_matrix, precision=lax.Precision...  9.11 us
    all_to_all x2, starting transfers between devices, per_device(): lax.all_to_all(mirrored, 'grp', split_axis=1, concat_axis=0, tiled=True)  7.98 us
    dot_general x3, matrix products, pair_kernel(): jnp.einsum('acp,bcp->abp', left_img, right_img, preferred_element_type=jn...  4.73 us
    ppermute x4, starting transfers between devices, shifted(): return lax.ppermute(block, axis, route)  4.28 us
    ppermute x4, waiting for transfers between devices, shifted(): return lax.ppermute(block, axis, route)  3.33 us
  transfers between devices with their start and end apart: 6, of which 4 were waited for; matrix products, arithmetic and copies ran while one was open for 21% of the time, Pallas kernels for 0%

commit v1 on v0

v1 whole, which is shorter than its diff:
```python
import functools
import math

import jax
import jax.numpy as jnp
from jax import lax
from jax.experimental import pallas as pl
from jax.experimental.pallas import tpu as pltpu
from jax.sharding import PartitionSpec as P

SIDE = 32
LAYERS = 3
ROUNDS = 2
SPAN = 2 * ROUNDS + 1
LANES = 128
ROWS = 8
BIAS = 0.1
MESH = pl.DeviceIdType.MESH

ARC = (
    0.31830988122327397,
    -0.022534660160951844,
    0.005977264482236005,
    -0.0024073736878517066,
    0.0010804572825488274,
    -0.0003963123703673673,
    7.618722193421786e-05,
)


def stencil_sum(maps, masks):
    first, last, not_left, not_right = masks
    chunks = len(maps)
    down = [pltpu.roll(x, SIDE, 1) for x in maps]
    up = [pltpu.roll(x, LANES - SIDE, 1) for x in maps]
    sums = []
    for k in range(chunks):
        above = jnp.where(first, down[k - 1] if k else 0.0, down[k])
        below = jnp.where(last, up[k + 1] if k < chunks - 1 else 0.0, up[k])
        sums.append(maps[k] + above + below)
    out = []
    for x in sums:
        left = jnp.where(not_left, pltpu.roll(x, 1, 1), 0.0)
        right = jnp.where(not_right, pltpu.roll(x, LANES - 1, 1), 0.0)
        out.append(x + left + right)
    return out


def lane_masks():
    lane = lax.broadcasted_iota(jnp.int32, (ROWS, LANES), 1)
    col = lane % SIDE
    return lane < SIDE, lane >= LANES - SIDE, col != 0, col != SIDE - 1


def channel_sum(terms):
    total = terms[0]
    for term in terms[1:]:
        total = total + term
    return total


def variance_roots(squares, channels, masks):
    current = [x * (1.0 / (9 * channels)) + BIAS for x in stencil_sum(squares, masks)]
    layers = []
    for layer in range(LAYERS):
        inverse = [lax.rsqrt(x) for x in current]
        layers.append(([x * y for x, y in zip(current, inverse)], inverse))
        if layer < LAYERS - 1:
            current = [x * (1.0 / 9) + BIAS for x in stencil_sum(current, masks)]
    return layers


def twice_relu(cov, scale, inverse):
    a = jnp.minimum(jnp.abs(cov) * inverse, 1.0)
    y = jnp.maximum(1.0 - a, 1e-30)
    poly = ARC[-1]
    for c in ARC[-2::-1]:
        poly = poly * a + c
    bent = y * y * lax.rsqrt(y) * poly
    return scale * bent + jnp.minimum(jnp.maximum(cov, 0.0), scale)


def kernel(
    n_blk, n_grp, images, out, got, own, flat, root, inv, wide, res,
    grp_send, grp_recv, blk_send, blk_recv,
):
    b, z = lax.axis_index("blk"), lax.axis_index("grp")
    chan, per, pix = images.shape
    chunks = pix // LANES
    image_rows = chan * chunks
    block = per * n_grp
    units = block // ROWS
    sources = ROWS // per
    offsets = [d for d in range(-ROUNDS, ROUNDS + 1) if d]

    barrier = pltpu.get_barrier_semaphore()
    for dz in range(1, n_grp):
        pl.semaphore_signal(
            barrier, inc=1, device_id={"grp": lax.rem(z + dz, n_grp)}, device_id_type=MESH
        )
    for d in offsets:
        pl.semaphore_signal(
            barrier, inc=1, device_id={"blk": lax.rem(b + d + n_blk, n_blk)}, device_id_type=MESH
        )

    data = images[...].astype(jnp.float32)
    for i in range(per):
        for k in range(chunks):
            flat[pl.ds(i * image_rows + k, chan, stride=chunks), :] = data[
                :, i, k * LANES : (k + 1) * LANES
            ]
    got[ROUNDS, z] = flat[...].astype(jnp.bfloat16)

    pl.semaphore_wait(barrier, n_grp - 1 + len(offsets))

    copies = []
    for dz in range(1, n_grp):
        copy = pltpu.make_async_remote_copy(
            src_ref=got.at[ROUNDS, z],
            dst_ref=got.at[ROUNDS, z],
            send_sem=grp_send.at[dz],
            recv_sem=grp_recv.at[z],
            device_id={"grp": lax.rem(z + dz, n_grp)},
            device_id_type=MESH,
        )
        copy.start()
        copies.append(copy)

    def pass_on(source, order):
        for at, d in enumerate(offsets):
            copy = pltpu.make_async_remote_copy(
                src_ref=got.at[ROUNDS, source],
                dst_ref=got.at[ROUNDS + d, source],
                send_sem=blk_send.at[order, at],
                recv_sem=blk_recv.at[ROUNDS + d, source],
                device_id={"blk": lax.rem(b - d + n_blk, n_blk)},
                device_id_type=MESH,
            )
            copy.start()
            copies.append(copy)

    pass_on(z, 0)

    masks = lane_masks()
    for i in range(per):
        squares = []
        for k in range(chunks):
            parts = []
            for c in range(chan):
                row = i * image_rows + c * chunks + k
                part = jnp.broadcast_to(flat[row : row + 1, :], (ROWS, LANES))
                own[row] = part
                parts.append(part * part)
            squares.append(channel_sum(parts))
        for layer, (roots, inverses) in enumerate(variance_roots(squares, chan, masks)):
            for k in range(chunks):
                at = (i * LAYERS + layer) * chunks + k
                root[at] = roots[k]
                inv[at] = inverses[k]

    def arrived(k, source, sem):
        pltpu.make_async_remote_copy(
            src_ref=got.at[k, source],
            dst_ref=got.at[k, source],
            send_sem=grp_send.at[0],
            recv_sem=sem,
            device_id={"grp": z},
            device_id_type=MESH,
        ).wait_recv()

    for dz in range(1, n_grp):
        source = lax.rem(z + dz, n_grp)
        arrived(ROUNDS, source, grp_recv.at[source])
        pass_on(source, dz)

    def one_unit(k, unit):
        for s in range(sources):
            wide[s * per * image_rows : (s + 1) * per * image_rows, :] = got[
                k, unit * sources + s
            ].astype(jnp.float32)
        theirs = [
            [wide[pl.ds(c * chunks + j, ROWS, stride=image_rows), :] for c in range(chan)]
            for j in range(chunks)
        ]
        layers = variance_roots(
            [channel_sum([x * x for x in parts]) for parts in theirs], chan, masks
        )
        for i in range(per):
            cov = [
                channel_sum(
                    [own[i * image_rows + c * chunks + j] * theirs[j][c] for c in range(chan)]
                )
                for j in range(chunks)
            ]
            factor = 1.0 / (9 * chan)
            for layer in range(LAYERS):
                at = (i * LAYERS + layer) * chunks
                roots, inverses = layers[layer]
                cov = [x * factor + BIAS for x in stencil_sum(cov, masks)]
                cov = [
                    twice_relu(cov[j], root[at + j] * roots[j], inv[at + j] * inverses[j])
                    for j in range(chunks)
                ]
                factor = 1.0 / 9
            at = ((i * SPAN + k) * units + unit) * ROWS
            res[pl.ds(pl.multiple_of(at, ROWS), ROWS), :] = channel_sum(cov)

    def one_block(t, carry):
        half = (t + 1) // 2
        k = ROUNDS + half * (1 - 2 * (t % 2))

        @pl.when(t > 0)
        def _():
            for source in range(n_grp):
                arrived(k, source, blk_recv.at[k, source])

        for unit in range(units):
            one_unit(k, unit)
        return carry

    lax.fori_loop(0, SPAN, one_block, 0)

    sums = lax.dot_general(
        jnp.full((ROWS, LANES), 1.0 / pix, jnp.float32),
        res[...],
        (((1,), (1,)), ((), ())),
        precision=lax.Precision.HIGHEST,
        preferred_element_type=jnp.float32,
    )
    out[...] = sums[0:1, :]
    for copy in copies:
        copy.wait_send()


def per_device(n_blk, n_grp, images):
    per, chan, pix = images.shape
    chunks = pix // LANES
    rows = per * chan * chunks
    block = per * n_grp
    assert block % ROWS == 0 and ROWS % per == 0
    total = per * SPAN * block
    maps = per * LAYERS * chunks
    sums = pl.pallas_call(
        functools.partial(kernel, n_blk, n_grp),
        out_shape=jax.ShapeDtypeStruct((1, total), jnp.float32),
        in_specs=[pl.BlockSpec(memory_space=pltpu.VMEM)],
        out_specs=pl.BlockSpec(memory_space=pltpu.VMEM),
        scratch_shapes=[
            pltpu.VMEM((SPAN, n_grp, rows, LANES), jnp.bfloat16),
            pltpu.VMEM((rows, ROWS, LANES), jnp.float32),
            pltpu.VMEM((rows, LANES), jnp.float32),
            pltpu.VMEM((maps, ROWS, LANES), jnp.float32),
            pltpu.VMEM((maps, ROWS, LANES), jnp.float32),
            pltpu.VMEM((ROWS * chan * chunks, LANES), jnp.float32),
            pltpu.VMEM((total, LANES), jnp.float32),
            pltpu.SemaphoreType.DMA((n_grp,)),
            pltpu.SemaphoreType.DMA((n_grp,)),
            pltpu.SemaphoreType.DMA((n_grp, SPAN - 1)),
            pltpu.SemaphoreType.DMA((SPAN, n_grp)),
        ],
        compiler_params=pltpu.CompilerParams(
            collective_id=0, has_side_effects=True, vmem_limit_bytes=16 * 1024 * 1024
        ),
    )(jnp.transpose(images, (1, 0, 2)))
    return sums.reshape(per, SPAN, block)


def solution(mesh):
    spec = P(("blk", "grp"), None, None)
    body = functools.partial(per_device, mesh.shape["blk"], mesh.shape["grp"])
    return jax.shard_map(body, mesh=mesh, in_specs=(spec,), out_specs=spec, check_vma=False)
```

time: 78.3 us -> 17 us (0.22)
  matrix products: 24.5 us -> 0 us
  blocking collectives: 14.9 us -> 0 us
  Pallas kernels: 0 us -> 14.2 us
  waiting for transfers between devices: 13.3 us -> 0 us
  starting transfers between devices: 12.3 us -> 0 us
  local copies, waits for them, and re-layouts: 11.5 us -> 1.9 us
    dot_general x45 -> x0, matrix products: 24.5 us -> none  [the longest x21 10.7 us: stencil_maps(): jnp.einsum('ab,...bc->...ac', band_matrix, shaped, precision=lax.Precisio...]
    all_gather x1 -> x0, blocking collectives: 14.9 us -> none  [per_device(): whole_block = lax.all_gather(images, 'grp', axis=0, tiled=True)]
    pallas_call x0 -> x1, Pallas kernels: none -> 14.2 us  [per_device(): pl.pallas_call(functools.partial(kernel, n_blk, n_grp), out_shape=jax.Sha...]
    all_to_all x2 -> x0, waiting for transfers between devices: 9.97 us -> none  [per_device(): lax.all_to_all(mirrored, 'grp', split_axis=1, concat_axis=0, tiled=True)]
    all_to_all x2 -> x0, starting transfers between devices: 7.98 us -> none  [per_device(): lax.all_to_all(mirrored, 'grp', split_axis=1, concat_axis=0, tiled=True)]
    ppermute x4 -> x0, starting transfers between devices: 4.28 us -> none  [shifted(): return lax.ppermute(block, axis, route)]
    ppermute x4 -> x0, waiting for transfers between devices: 3.33 us -> none  [shifted(): return lax.ppermute(block, axis, route)]
    unnamed x12 -> x2, local copies, waits for them, and re-layouts: 3.16 us -> 0.71 us
  transfers between devices with their start and end apart: 6 -> 0, of which waited for: 4 -> 0; matrix products, arithmetic and copies ran while one was open for 21% -> 0% of each run, Pallas kernels for 0% -> 0%
where the time goes in v1:
time: 17 us; the launch traced here: 16.8 us
  Pallas kernels  14.2 us (84%)
  local copies, waits for them, and re-layouts  1.9 us (11%)
  other arithmetic  0.66 us (4%)
    pallas_call x1, Pallas kernels, per_device(): pl.pallas_call(functools.partial(kernel, n_blk, n_grp), out_shape=jax.Sha...  14.2 us
    unnamed x2, local copies, waits for them, and re-layouts  0.71 us
    reshape x2, local copies, waits for them, and re-layouts, per_device(): return sums.reshape(per, SPAN, block)  0.68 us
    pallas_call x1, other arithmetic, per_device(): pl.pallas_call(functools.partial(kernel, n_blk, n_grp), out_shape=jax.Sha...  0.66 us
    pallas_call x1, local copies, waits for them, and re-layouts, per_device(): pl.pallas_call(functools.partial(kernel, n_blk, n_grp), out_shape=jax.Sha...  0.51 us

profile of v1, /device:TPU:0, one launch (start us, length us, event | category | flops | bytes accessed | tf_op | source)
XLA Modules:
  0.0 16.8 jit_solution(4854416773518939808)
XLA Ops:
  0.0 0.0 copy-start
  0.0 0.7 %copy-done = bf16[2,3,1024]{2,0,1:T(2,128)(2,1)S(1)} copy-done((bf16[2,3,1024]{2,0,1:T(2,128)(2,1)S(1)}, bf16[2,3,1024]{2,0,1:T(2,128)(2,1)}, u32[]{:S(2)}) %copy-start) | copy-done | bytes 12312
  0.7 14.2 %shard_map.17 = f32[1,80]{1,0:T(1,128)S(1)} custom-call(bf16[3,2,1024]{2,1,0:T(2,128)(2,1)S(1)} %bitcast.1), custom_call_target="tpu_custom_call" | custom-call | tf_op jit(solution)/shard_map/pallas_call | solution.py:243
  14.9 0.5 %broadcast.3 = f32[]{:T(128)} broadcast(f32[]{:T(128)} %constant.4), dimensions={} | broadcast | bytes 8 | tf_op jit(solution)/shard_map/pallas_call | solution.py:243
  15.5 0.7 %reduce.3 = f32[80]{0:T(128)S(1)} reduce(f32[1,80]{1,0:T(1,128)S(1)} %shard_map.17, f32[]{:T(128)} %broadcast.3), dimensions={0}, to_apply=%pallas_call.3.reduce_sub_computation.3 | reduce | bytes 644 | tf_op jit(solution)/shard_map/pallas_call | solution.py:243
  16.1 0.1 reshape.3
  16.2 0.6 %copy.3 = f32[2,5,8]{2,0,1:T(2,128)} copy(f32[2,5,8]{2,1,0:T(8,128)S(1)} %reshape.3) | data formatting | bytes 640 | tf_op jit(solution)/shard_map/reshape | solution.py:265
Async XLA Ops:
  0.0 0.7 %copy-start = (bf16[2,3,1024]{2,0,1:T(2,128)(2,1)S(1)}, bf16[2,3,1024]{2,0,1:T(2,128)(2,1)}, u32[]{:S(2)}) copy-start(bf16[2,3,1024]{2,0,1:T(2,128)(2,1)} %param.1) | copy-start | bytes 36868

commit v2 on v1

--- a/solution.py
+++ b/solution.py
@@ -1,5 +1,4 @@
 import functools
-import math
 
 import jax
 import jax.numpy as jnp
@@ -15,16 +14,16 @@
 LANES = 128
 ROWS = 8
 BIAS = 0.1
+BELOW_ONE = 1.0 - 2.0**-24
 MESH = pl.DeviceIdType.MESH
 
 ARC = (
-    0.31830988122327397,
-    -0.022534660160951844,
-    0.005977264482236005,
-    -0.0024073736878517066,
-    0.0010804572825488274,
-    -0.0003963123703673673,
-    7.618722193421786e-05,
+    0.3183098449892848,
+    -0.02253203775558662,
+    0.005946535585369838,
+    -0.002275705294168609,
+    0.0008254564785290766,
+    -0.00016869743862866002,
 )
 
 
@@ -71,8 +70,8 @@
 
 
 def twice_relu(cov, scale, inverse):
-    a = jnp.minimum(jnp.abs(cov) * inverse, 1.0)
-    y = jnp.maximum(1.0 - a, 1e-30)
+    a = jnp.minimum(jnp.abs(cov) * inverse, BELOW_ONE)
+    y = 1.0 - a
     poly = ARC[-1]
     for c in ARC[-2::-1]:
         poly = poly * a + c
@@ -81,8 +80,8 @@
 
 
 def kernel(
-    n_blk, n_grp, images, out, got, own, flat, root, inv, wide, res,
-    grp_send, grp_recv, blk_send, blk_recv,
+    n_blk, n_grp, images, out, raw, got, own, flat, root, inv, wide, res,
+    raw_sem, grp_send, grp_recv, blk_send, blk_recv,
 ):
     b, z = lax.axis_index("blk"), lax.axis_index("grp")
     chan, per, pix = images.shape
@@ -93,6 +92,8 @@
     sources = ROWS // per
     offsets = [d for d in range(-ROUNDS, ROUNDS + 1) if d]
 
+    load = pltpu.make_async_copy(images, raw, raw_sem)
+    load.start()
     barrier = pltpu.get_barrier_semaphore()
     for dz in range(1, n_grp):
         pl.semaphore_signal(
@@ -102,8 +103,9 @@
         pl.semaphore_signal(
             barrier, inc=1, device_id={"blk": lax.rem(b + d + n_blk, n_blk)}, device_id_type=MESH
         )
-
-    data = images[...].astype(jnp.float32)
+    load.wait()
+
+    data = raw[...].astype(jnp.float32)
     for i in range(per):
         for k in range(chunks):
             flat[pl.ds(i * image_rows + k, chan, stride=chunks), :] = data[
@@ -173,10 +175,10 @@
         arrived(ROUNDS, source, grp_recv.at[source])
         pass_on(source, dz)
 
-    def one_unit(k, unit):
-        for s in range(sources):
+    def one_unit(places, slot):
+        for s, (k, source) in enumerate(places):
             wide[s * per * image_rows : (s + 1) * per * image_rows, :] = got[
-                k, unit * sources + s
+                k, source
             ].astype(jnp.float32)
         theirs = [
             [wide[pl.ds(c * chunks + j, ROWS, stride=image_rows), :] for c in range(chan)]
@@ -202,32 +204,51 @@
                     for j in range(chunks)
                 ]
                 factor = 1.0 / 9
-            at = ((i * SPAN + k) * units + unit) * ROWS
-            res[pl.ds(pl.multiple_of(at, ROWS), ROWS), :] = channel_sum(cov)
-
-    def one_block(t, carry):
-        half = (t + 1) // 2
-        k = ROUNDS + half * (1 - 2 * (t % 2))
-
-        @pl.when(t > 0)
+            res[i, slot] = channel_sum(cov)
+
+    def step(t, carry):
+        home = ((t >= 1) & (t <= units)).astype(jnp.int32)
+        away = 1 - home
+        order = jnp.where(t > units, t - units, 0)
+        source = lax.rem(z + order, n_grp)
+
+        @pl.when(home == 0)
         def _():
-            for source in range(n_grp):
-                arrived(k, source, blk_recv.at[k, source])
-
+            for d in offsets:
+                arrived(ROUNDS + d, source, blk_recv.at[ROUNDS + d, source])
+
+        unit = home * (t - 1)
+        one_unit(
+            [
+                (ROUNDS + away * d, away * source + home * (unit * sources + s))
+                for s, d in enumerate(offsets)
+            ],
+            home * unit + away * (units + source),
+        )
+        return carry
+
+    lax.fori_loop(0, units + n_grp, step, 0)
+
+    row = lax.broadcasted_iota(jnp.int32, (ROWS, LANES), 0)
+    lane = lax.broadcasted_iota(jnp.int32, (ROWS, LANES), 1)
+    for i in range(per):
+        sums = [
+            jnp.sum(res[i, slot], axis=1, keepdims=True) * (1.0 / pix)
+            for slot in range(units + n_grp)
+        ]
+        home = jnp.zeros((ROWS, LANES), jnp.float32)
         for unit in range(units):
-            one_unit(k, unit)
-        return carry
-
-    lax.fori_loop(0, SPAN, one_block, 0)
-
-    sums = lax.dot_general(
-        jnp.full((ROWS, LANES), 1.0 / pix, jnp.float32),
-        res[...],
-        (((1,), (1,)), ((), ())),
-        precision=lax.Precision.HIGHEST,
-        preferred_element_type=jnp.float32,
-    )
-    out[...] = sums[0:1, :]
+            home = jnp.where(lane == row + unit * ROWS, sums[unit], home)
+        out[ROUNDS, i : i + 1, :] = jnp.sum(home, axis=0, keepdims=True)[:, :block]
+        away = jnp.zeros((ROWS, LANES), jnp.float32)
+        for source in range(n_grp):
+            mine = (lane // per == source) & (lane % per == row % per)
+            away = jnp.where(mine, sums[units + source], away)
+        total = away
+        for r in range(1, per):
+            total = total + pltpu.roll(away, ROWS - r, 0)
+        for at, d in enumerate(offsets):
+            out[ROUNDS + d, i : i + 1, :] = total[at * per : at * per + 1, :block]
     for copy in copies:
         copy.wait_send()
 
@@ -237,32 +258,33 @@
     chunks = pix // LANES
     rows = per * chan * chunks
     block = per * n_grp
-    assert block % ROWS == 0 and ROWS % per == 0
-    total = per * SPAN * block
+    assert block % ROWS == 0 and per * (SPAN - 1) == ROWS
     maps = per * LAYERS * chunks
-    sums = pl.pallas_call(
+    window = pl.pallas_call(
         functools.partial(kernel, n_blk, n_grp),
-        out_shape=jax.ShapeDtypeStruct((1, total), jnp.float32),
-        in_specs=[pl.BlockSpec(memory_space=pltpu.VMEM)],
+        out_shape=jax.ShapeDtypeStruct((SPAN, per, block), jnp.float32),
+        in_specs=[pl.BlockSpec(memory_space=pltpu.HBM)],
         out_specs=pl.BlockSpec(memory_space=pltpu.VMEM),
         scratch_shapes=[
+            pltpu.VMEM((chan, per, pix), jnp.bfloat16),
             pltpu.VMEM((SPAN, n_grp, rows, LANES), jnp.bfloat16),
             pltpu.VMEM((rows, ROWS, LANES), jnp.float32),
             pltpu.VMEM((rows, LANES), jnp.float32),
             pltpu.VMEM((maps, ROWS, LANES), jnp.float32),
             pltpu.VMEM((maps, ROWS, LANES), jnp.float32),
             pltpu.VMEM((ROWS * chan * chunks, LANES), jnp.float32),
-            pltpu.VMEM((total, LANES), jnp.float32),
+            pltpu.VMEM((per, block // ROWS + n_grp, ROWS, LANES), jnp.float32),
+            pltpu.SemaphoreType.DMA,
             pltpu.SemaphoreType.DMA((n_grp,)),
             pltpu.SemaphoreType.DMA((n_grp,)),
             pltpu.SemaphoreType.DMA((n_grp, SPAN - 1)),
             pltpu.SemaphoreType.DMA((SPAN, n_grp)),
         ],
         compiler_params=pltpu.CompilerParams(
-            collective_id=0, has_side_effects=True, vmem_limit_bytes=16 * 1024 * 1024
+            collective_id=0, has_side_effects=True, vmem_limit_bytes=32 * 1024 * 1024
         ),
     )(jnp.transpose(images, (1, 0, 2)))
-    return sums.reshape(per, SPAN, block)
+    return jnp.transpose(window, (1, 0, 2))
 
 
 def solution(mesh):

time: 17 us -> 15.5 us (0.912)
  other arithmetic: 0.66 us -> 0 us
  local copies, waits for them, and re-layouts: 1.9 us -> 1.3 us
  Pallas kernels: 14.2 us -> 14 us
    reshape x2 -> x0, local copies, waits for them, and re-layouts: 0.68 us -> none  [per_device(): return sums.reshape(per, SPAN, block)]
    pallas_call x1 -> x0, other arithmetic: 0.66 us -> none  [per_device(): pl.pallas_call(functools.partial(kernel, n_blk, n_grp), out_shape=jax.Sha...]
    unnamed x2 -> x3, local copies, waits for them, and re-layouts: 0.71 us -> 1.3 us
    pallas_call x1 -> x0, local copies, waits for them, and re-layouts: 0.51 us -> none  [per_device(): pl.pallas_call(functools.partial(kernel, n_blk, n_grp), out_shape=jax.Sha...]
    pallas_call x1, Pallas kernels: 14.2 us -> 14 us  [per_device(): pl.pallas_call(functools.partial(kernel, n_blk, n_grp), out_shape=jax.Sha...]
where the time goes in v2:
time: 15.5 us; the launch traced here: 15.3 us
  Pallas kernels  14 us (90%)
  local copies, waits for them, and re-layouts  1.3 us (8%)
    pallas_call x1, Pallas kernels, per_device(): pl.pallas_call(functools.partial(kernel, n_blk, n_grp), out_shape=jax.Sha...  14 us
    unnamed x3, local copies, waits for them, and re-layouts  1.3 us

profile of v2, /device:TPU:0, one launch (start us, length us, event | category | flops | bytes accessed | tf_op | source)
XLA Modules:
  0.0 15.3 jit_solution(9334071941729639876)
XLA Ops:
  0.0 0.0 copy-start
  0.0 0.7 %copy-done = bf16[2,3,1024]{2,0,1:T(2,128)(2,1)S(1)} copy-done((bf16[2,3,1024]{2,0,1:T(2,128)(2,1)S(1)}, bf16[2,3,1024]{2,0,1:T(2,128)(2,1)}, u32[]{:S(2)}) %copy-start) | copy-done | bytes 12312
  0.7 14.0 %shard_map.17 = f32[5,2,8]{2,1,0:T(2,128)S(1)} custom-call(bf16[3,2,1024]{2,1,0:T(2,128)(2,1)S(1)} %bitcast.3), custom_call_target="tpu_custom_call" | custom-call | tf_op jit(solution)/shard_map/pallas_call | solution.py:263
  14.7 0.6 %copy.3 = f32[2,5,8]{2,0,1:T(2,128)} copy(f32[2,5,8]{2,0,1:T(2,128)S(1)} %bitcast.2) | data formatting | bytes 640
Async XLA Ops:
  0.0 0.7 %copy-start = (bf16[2,3,1024]{2,0,1:T(2,128)(2,1)S(1)}, bf16[2,3,1024]{2,0,1:T(2,128)(2,1)}, u32[]{:S(2)}) copy-start(bf16[2,3,1024]{2,0,1:T(2,128)(2,1)} %param.1) | copy-start | bytes 36868

commit v3 on v2

--- a/solution.py
+++ b/solution.py
@@ -27,21 +27,20 @@
 )
 
 
-def stencil_sum(maps, masks):
+def stencil_sum(groups, masks):
     first, last, not_left, not_right = masks
-    chunks = len(maps)
-    down = [pltpu.roll(x, SIDE, 1) for x in maps]
-    up = [pltpu.roll(x, LANES - SIDE, 1) for x in maps]
-    sums = []
-    for k in range(chunks):
-        above = jnp.where(first, down[k - 1] if k else 0.0, down[k])
-        below = jnp.where(last, up[k + 1] if k < chunks - 1 else 0.0, up[k])
-        sums.append(maps[k] + above + below)
+    tall = []
+    for maps in groups:
+        above = jnp.where(first, 0.0, pltpu.roll(maps[-1], SIDE, 1))
+        below = jnp.where(last, 0.0, pltpu.roll(maps[0], LANES - SIDE, 1))
+        column = [above] + list(maps) + [below]
+        pairs = [x + y for x, y in zip(column[:-1], column[1:])]
+        tall.append([pairs[k] + column[k + 2] for k in range(len(maps))])
     out = []
-    for x in sums:
-        left = jnp.where(not_left, pltpu.roll(x, 1, 1), 0.0)
-        right = jnp.where(not_right, pltpu.roll(x, LANES - 1, 1), 0.0)
-        out.append(x + left + right)
+    for maps in tall:
+        left = [jnp.where(not_left, pltpu.roll(x, 1, 1), 0.0) for x in maps]
+        right = [jnp.where(not_right, pltpu.roll(x, LANES - 1, 1), 0.0) for x in maps]
+        out.append([x + (y + z) for x, y, z in zip(maps, left, right)])
     return out
 
 
@@ -58,15 +57,13 @@
     return total
 
 
-def variance_roots(squares, channels, masks):
-    current = [x * (1.0 / (9 * channels)) + BIAS for x in stencil_sum(squares, masks)]
-    layers = []
-    for layer in range(LAYERS):
-        inverse = [lax.rsqrt(x) for x in current]
-        layers.append(([x * y for x, y in zip(current, inverse)], inverse))
-        if layer < LAYERS - 1:
-            current = [x * (1.0 / 9) + BIAS for x in stencil_sum(current, masks)]
-    return layers
+def affine(groups, factor):
+    return [[x * factor + BIAS for x in maps] for maps in groups]
+
+
+def roots_of(maps):
+    inverse = [lax.rsqrt(x) for x in maps]
+    return [x * y for x, y in zip(maps, inverse)], inverse
 
 
 def twice_relu(cov, scale, inverse):
@@ -80,7 +77,7 @@
 
 
 def kernel(
-    n_blk, n_grp, images, out, raw, got, own, flat, root, inv, wide, res,
+    n_blk, n_grp, images, out, raw, turn, got, own, flat, root, inv, wide, res,
     raw_sem, grp_send, grp_recv, blk_send, blk_recv,
 ):
     b, z = lax.axis_index("blk"), lax.axis_index("grp")
@@ -106,11 +103,23 @@
     load.wait()
 
     data = raw[...].astype(jnp.float32)
-    for i in range(per):
-        for k in range(chunks):
-            flat[pl.ds(i * image_rows + k, chan, stride=chunks), :] = data[
-                :, i, k * LANES : (k + 1) * LANES
+    for k in range(chunks):
+        for c in range(chan):
+            turn[pl.ds(k * ROWS + c, per, stride=chan), :] = data[
+                c, :, k * LANES : (k + 1) * LANES
             ]
+    lane = lax.broadcasted_iota(jnp.int32, (ROWS, LANES), 1)
+    natural = [turn[k * ROWS : (k + 1) * ROWS, :] for k in range(chunks)]
+    fold = LANES // SIDE
+    for k in range(chunks):
+        row = None
+        for g in range(fold):
+            at = g * chunks + k
+            part = natural[at // fold]
+            shift = (g - at % fold) * SIDE % LANES
+            part = pltpu.roll(part, shift, 1) if shift else part
+            row = part if row is None else jnp.where(lane >= g * SIDE, part, row)
+        flat[pl.ds(k, per * chan, stride=chunks), :] = row[: per * chan]
     got[ROUNDS, z] = flat[...].astype(jnp.bfloat16)
 
     pl.semaphore_wait(barrier, n_grp - 1 + len(offsets))
@@ -144,6 +153,7 @@
     pass_on(z, 0)
 
     masks = lane_masks()
+    current = []
     for i in range(per):
         squares = []
         for k in range(chunks):
@@ -154,7 +164,12 @@
                 own[row] = part
                 parts.append(part * part)
             squares.append(channel_sum(parts))
-        for layer, (roots, inverses) in enumerate(variance_roots(squares, chan, masks)):
+        current.append(squares)
+    for layer in range(LAYERS):
+        factor = 1.0 / 9 if layer else 1.0 / (9 * chan)
+        current = affine(stencil_sum(current, masks), factor)
+        for i in range(per):
+            roots, inverses = roots_of(current[i])
             for k in range(chunks):
                 at = (i * LAYERS + layer) * chunks + k
                 root[at] = roots[k]
@@ -175,39 +190,48 @@
         arrived(ROUNDS, source, grp_recv.at[source])
         pass_on(source, dz)
 
-    def one_unit(places, slot):
-        for s, (k, source) in enumerate(places):
-            wide[s * per * image_rows : (s + 1) * per * image_rows, :] = got[
-                k, source
-            ].astype(jnp.float32)
-        theirs = [
-            [wide[pl.ds(c * chunks + j, ROWS, stride=image_rows), :] for c in range(chan)]
-            for j in range(chunks)
-        ]
-        layers = variance_roots(
-            [channel_sum([x * x for x in parts]) for parts in theirs], chan, masks
-        )
-        for i in range(per):
-            cov = [
-                channel_sum(
-                    [own[i * image_rows + c * chunks + j] * theirs[j][c] for c in range(chan)]
-                )
+    def work(members):
+        maps = []
+        for m, (places, slot) in enumerate(members):
+            for s, (k, source) in enumerate(places):
+                wide[m, s * per * image_rows : (s + 1) * per * image_rows, :] = got[
+                    k, source
+                ].astype(jnp.float32)
+            theirs = [
+                [wide[m, pl.ds(c * chunks + j, ROWS, stride=image_rows), :] for c in range(chan)]
                 for j in range(chunks)
             ]
-            factor = 1.0 / (9 * chan)
-            for layer in range(LAYERS):
-                at = (i * LAYERS + layer) * chunks
-                roots, inverses = layers[layer]
-                cov = [x * factor + BIAS for x in stencil_sum(cov, masks)]
-                cov = [
-                    twice_relu(cov[j], root[at + j] * roots[j], inv[at + j] * inverses[j])
-                    for j in range(chunks)
-                ]
-                factor = 1.0 / 9
-            res[i, slot] = channel_sum(cov)
-
-    def step(t, carry):
-        home = ((t >= 1) & (t <= units)).astype(jnp.int32)
+            maps.append([channel_sum([x * x for x in parts]) for parts in theirs])
+            for i in range(per):
+                maps.append(
+                    [
+                        channel_sum(
+                            [
+                                own[i * image_rows + c * chunks + j] * theirs[j][c]
+                                for c in range(chan)
+                            ]
+                        )
+                        for j in range(chunks)
+                    ]
+                )
+        for layer in range(LAYERS):
+            factor = 1.0 / 9 if layer else 1.0 / (9 * chan)
+            maps = affine(stencil_sum(maps, masks), factor)
+            for m in range(len(members)):
+                roots, inverses = roots_of(maps[m * (per + 1)])
+                for i in range(per):
+                    at = (i * LAYERS + layer) * chunks
+                    cov = maps[m * (per + 1) + 1 + i]
+                    maps[m * (per + 1) + 1 + i] = [
+                        twice_relu(cov[j], root[at + j] * roots[j], inv[at + j] * inverses[j])
+                        for j in range(chunks)
+                    ]
+        for m, (places, slot) in enumerate(members):
+            for i in range(per):
+                res[i, slot] = channel_sum(maps[m * (per + 1) + 1 + i])
+
+    def member(t):
+        home = jnp.int32((t >= 1) & (t <= units))
         away = 1 - home
         order = jnp.where(t > units, t - units, 0)
         source = lax.rem(z + order, n_grp)
@@ -218,16 +242,21 @@
                 arrived(ROUNDS + d, source, blk_recv.at[ROUNDS + d, source])
 
         unit = home * (t - 1)
-        one_unit(
-            [
-                (ROUNDS + away * d, away * source + home * (unit * sources + s))
-                for s, d in enumerate(offsets)
-            ],
-            home * unit + away * (units + source),
-        )
+        places = [
+            (ROUNDS + away * d, away * source + home * (unit * sources + s))
+            for s, d in enumerate(offsets)
+        ]
+        return places, home * unit + away * (units + source)
+
+    total_units = units + n_grp
+
+    def step(t, carry):
+        work([member(2 * t), member(2 * t + 1)])
         return carry
 
-    lax.fori_loop(0, units + n_grp, step, 0)
+    lax.fori_loop(0, total_units // 2, step, 0)
+    if total_units % 2:
+        work([member(jnp.int32(total_units - 1))])
 
     row = lax.broadcasted_iota(jnp.int32, (ROWS, LANES), 0)
     lane = lax.broadcasted_iota(jnp.int32, (ROWS, LANES), 1)
@@ -267,12 +296,13 @@
         out_specs=pl.BlockSpec(memory_space=pltpu.VMEM),
         scratch_shapes=[
             pltpu.VMEM((chan, per, pix), jnp.bfloat16),
+            pltpu.VMEM((chunks * ROWS, LANES), jnp.float32),
             pltpu.VMEM((SPAN, n_grp, rows, LANES), jnp.bfloat16),
             pltpu.VMEM((rows, ROWS, LANES), jnp.float32),
             pltpu.VMEM((rows, LANES), jnp.float32),
             pltpu.VMEM((maps, ROWS, LANES), jnp.float32),
             pltpu.VMEM((maps, ROWS, LANES), jnp.float32),
-            pltpu.VMEM((ROWS * chan * chunks, LANES), jnp.float32),
+            pltpu.VMEM((2, ROWS * chan * chunks, LANES), jnp.float32),
             pltpu.VMEM((per, block // ROWS + n_grp, ROWS, LANES), jnp.float32),
             pltpu.SemaphoreType.DMA,
             pltpu.SemaphoreType.DMA((n_grp,)),

time: 15.5 us -> 15.2 us (0.981)
  Pallas kernels: 14 us -> 13.7 us
    pallas_call x1, Pallas kernels: 14 us -> 13.7 us  [per_device(): pl.pallas_call(functools.partial(kernel, n_blk, n_grp), out_shape=jax.Sha...]
where the time goes in v3:
time: 15.2 us; the launch traced here: 15 us
  Pallas kernels  13.7 us (90%)
  local copies, waits for them, and re-layouts  1.3 us (9%)
    pallas_call x1, Pallas kernels, per_device(): pl.pallas_call(functools.partial(kernel, n_blk, n_grp), out_shape=jax.Sha...  13.7 us
    unnamed x3, local copies, waits for them, and re-layouts  1.3 us

profile of v3, /device:TPU:0, one launch (start us, length us, event | category | flops | bytes accessed | tf_op | source)
XLA Modules:
  0.0 15.0 jit_solution(9660696841948769284)
XLA Ops:
  0.0 0.0 copy-start
  0.0 0.7 %copy-done = bf16[2,3,1024]{2,0,1:T(2,128)(2,1)S(1)} copy-done((bf16[2,3,1024]{2,0,1:T(2,128)(2,1)S(1)}, bf16[2,3,1024]{2,0,1:T(2,128)(2,1)}, u32[]{:S(2)}) %copy-start) | copy-done | bytes 12312
  0.7 13.7 %shard_map.17 = f32[5,2,8]{2,1,0:T(2,128)S(1)} custom-call(bf16[3,2,1024]{2,1,0:T(2,128)(2,1)S(1)} %bitcast.3), custom_call_target="tpu_custom_call" | custom-call | tf_op jit(solution)/shard_map/pallas_call | solution.py:292
  14.4 0.6 %copy.3 = f32[2,5,8]{2,0,1:T(2,128)} copy(f32[2,5,8]{2,0,1:T(2,128)S(1)} %bitcast.2) | data formatting | bytes 640
Async XLA Ops:
  0.0 0.7 %copy-start = (bf16[2,3,1024]{2,0,1:T(2,128)(2,1)S(1)}, bf16[2,3,1024]{2,0,1:T(2,128)(2,1)}, u32[]{:S(2)}) copy-start(bf16[2,3,1024]{2,0,1:T(2,128)(2,1)} %param.1) | copy-start | bytes 36868

commit v4 on v3

--- a/solution.py
+++ b/solution.py
@@ -77,8 +77,8 @@
 
 
 def kernel(
-    n_blk, n_grp, images, out, raw, turn, got, own, flat, root, inv, wide, res,
-    raw_sem, grp_send, grp_recv, blk_send, blk_recv,
+    n_blk, n_grp, images, out, raw, turn, got, own, flat, root, inv, wide,
+    gone, back, raw_sem, grp_send, grp_recv, blk_send, blk_recv, gone_sem, back_sem,
 ):
     b, z = lax.axis_index("blk"), lax.axis_index("grp")
     chan, per, pix = images.shape
@@ -87,7 +87,7 @@
     block = per * n_grp
     units = block // ROWS
     sources = ROWS // per
-    offsets = [d for d in range(-ROUNDS, ROUNDS + 1) if d]
+    span = range(1, ROUNDS + 1)
 
     load = pltpu.make_async_copy(images, raw, raw_sem)
     load.start()
@@ -96,9 +96,9 @@
         pl.semaphore_signal(
             barrier, inc=1, device_id={"grp": lax.rem(z + dz, n_grp)}, device_id_type=MESH
         )
-    for d in offsets:
+    for d in span:
         pl.semaphore_signal(
-            barrier, inc=1, device_id={"blk": lax.rem(b + d + n_blk, n_blk)}, device_id_type=MESH
+            barrier, inc=1, device_id={"blk": lax.rem(b - d + n_blk, n_blk)}, device_id_type=MESH
         )
     load.wait()
 
@@ -120,15 +120,15 @@
             part = pltpu.roll(part, shift, 1) if shift else part
             row = part if row is None else jnp.where(lane >= g * SIDE, part, row)
         flat[pl.ds(k, per * chan, stride=chunks), :] = row[: per * chan]
-    got[ROUNDS, z] = flat[...].astype(jnp.bfloat16)
-
-    pl.semaphore_wait(barrier, n_grp - 1 + len(offsets))
+    got[0, z] = flat[...].astype(jnp.bfloat16)
+
+    pl.semaphore_wait(barrier, n_grp - 1 + ROUNDS)
 
     copies = []
     for dz in range(1, n_grp):
         copy = pltpu.make_async_remote_copy(
-            src_ref=got.at[ROUNDS, z],
-            dst_ref=got.at[ROUNDS, z],
+            src_ref=got.at[0, z],
+            dst_ref=got.at[0, z],
             send_sem=grp_send.at[dz],
             recv_sem=grp_recv.at[z],
             device_id={"grp": lax.rem(z + dz, n_grp)},
@@ -138,13 +138,13 @@
         copies.append(copy)
 
     def pass_on(source, order):
-        for at, d in enumerate(offsets):
+        for d in span:
             copy = pltpu.make_async_remote_copy(
-                src_ref=got.at[ROUNDS, source],
-                dst_ref=got.at[ROUNDS + d, source],
-                send_sem=blk_send.at[order, at],
-                recv_sem=blk_recv.at[ROUNDS + d, source],
-                device_id={"blk": lax.rem(b - d + n_blk, n_blk)},
+                src_ref=got.at[0, source],
+                dst_ref=got.at[d, source],
+                send_sem=blk_send.at[order, d - 1],
+                recv_sem=blk_recv.at[d - 1, source],
+                device_id={"blk": lax.rem(b + d, n_blk)},
                 device_id_type=MESH,
             )
             copy.start()
@@ -175,10 +175,10 @@
                 root[at] = roots[k]
                 inv[at] = inverses[k]
 
-    def arrived(k, source, sem):
+    def arrived(ref, sem):
         pltpu.make_async_remote_copy(
-            src_ref=got.at[k, source],
-            dst_ref=got.at[k, source],
+            src_ref=ref,
+            dst_ref=ref,
             send_sem=grp_send.at[0],
             recv_sem=sem,
             device_id={"grp": z},
@@ -187,12 +187,12 @@
 
     for dz in range(1, n_grp):
         source = lax.rem(z + dz, n_grp)
-        arrived(ROUNDS, source, grp_recv.at[source])
+        arrived(got.at[0, source], grp_recv.at[source])
         pass_on(source, dz)
 
     def work(members):
         maps = []
-        for m, (places, slot) in enumerate(members):
+        for m, places in enumerate(members):
             for s, (k, source) in enumerate(places):
                 wide[m, s * per * image_rows : (s + 1) * per * image_rows, :] = got[
                     k, source
@@ -226,58 +226,65 @@
                         twice_relu(cov[j], root[at + j] * roots[j], inv[at + j] * inverses[j])
                         for j in range(chunks)
                     ]
-        for m, (places, slot) in enumerate(members):
-            for i in range(per):
-                res[i, slot] = channel_sum(maps[m * (per + 1) + 1 + i])
-
-    def member(t):
-        home = jnp.int32((t >= 1) & (t <= units))
-        away = 1 - home
-        order = jnp.where(t > units, t - units, 0)
-        source = lax.rem(z + order, n_grp)
-
-        @pl.when(home == 0)
-        def _():
-            for d in offsets:
-                arrived(ROUNDS + d, source, blk_recv.at[ROUNDS + d, source])
-
-        unit = home * (t - 1)
-        places = [
-            (ROUNDS + away * d, away * source + home * (unit * sources + s))
-            for s, d in enumerate(offsets)
+        return [
+            [
+                jnp.sum(channel_sum(maps[m * (per + 1) + 1 + i]), axis=1, keepdims=True)
+                * (1.0 / pix)
+                for i in range(per)
+            ]
+            for m in range(len(members))
         ]
-        return places, home * unit + away * (units + source)
-
-    total_units = units + n_grp
-
-    def step(t, carry):
-        work([member(2 * t), member(2 * t + 1)])
-        return carry
-
-    lax.fori_loop(0, total_units // 2, step, 0)
-    if total_units % 2:
-        work([member(jnp.int32(total_units - 1))])
 
     row = lax.broadcasted_iota(jnp.int32, (ROWS, LANES), 0)
-    lane = lax.broadcasted_iota(jnp.int32, (ROWS, LANES), 1)
+
+    home = [jnp.zeros((ROWS, LANES), jnp.float32) for _ in range(per)]
+    for unit in range(units):
+        (sums,) = work([[(0, unit * sources + s) for s in range(sources)]])
+        for i in range(per):
+            home[i] = jnp.where(lane == row + unit * ROWS, sums[i], home[i])
     for i in range(per):
-        sums = [
-            jnp.sum(res[i, slot], axis=1, keepdims=True) * (1.0 / pix)
-            for slot in range(units + n_grp)
-        ]
-        home = jnp.zeros((ROWS, LANES), jnp.float32)
-        for unit in range(units):
-            home = jnp.where(lane == row + unit * ROWS, sums[unit], home)
-        out[ROUNDS, i : i + 1, :] = jnp.sum(home, axis=0, keepdims=True)[:, :block]
-        away = jnp.zeros((ROWS, LANES), jnp.float32)
+        out[ROUNDS, i : i + 1, :] = jnp.sum(home[i], axis=0, keepdims=True)[:, :block]
+
+    step = sources // ROUNDS
+    before = [jnp.zeros((ROWS, LANES), jnp.float32) for _ in range(per)]
+    for first in range(0, n_grp, step):
+        places = []
+        for a in range(step):
+            source = lax.rem(z + first + a, n_grp)
+            for d in span:
+                arrived(got.at[d, source], blk_recv.at[d - 1, source])
+                places.append((d, source))
+        (sums,) = work([places])
+        mirror = jnp.zeros((ROWS, LANES), jnp.float32)
+        for i in range(per):
+            mirror = jnp.where(lane == z * per + i, sums[i], mirror)
+        for s, (d, source) in enumerate(places):
+            at = first // step * sources + s
+            gone[at] = mirror[s * per : (s + 1) * per, :]
+            copy = pltpu.make_async_remote_copy(
+                src_ref=gone.at[at],
+                dst_ref=back.at[d - 1, z],
+                send_sem=gone_sem.at[at],
+                recv_sem=back_sem.at[d - 1, z],
+                device_id={"blk": lax.rem(b - d + n_blk, n_blk), "grp": source},
+                device_id_type=MESH,
+            )
+            copy.start()
+            copies.append(copy)
+        column = lax.rem(row, per) + per * lax.rem(z + first + row // (per * ROUNDS), n_grp)
+        for i in range(per):
+            before[i] = jnp.where(lane == column, sums[i], before[i])
+    place = lax.rem(row // per, ROUNDS)
+    for d in span:
+        for i in range(per):
+            mine = jnp.where(place == d - 1, before[i], 0.0)
+            out[ROUNDS - d, i : i + 1, :] = jnp.sum(mine, axis=0, keepdims=True)[:, :block]
+
+    for d in span:
         for source in range(n_grp):
-            mine = (lane // per == source) & (lane % per == row % per)
-            away = jnp.where(mine, sums[units + source], away)
-        total = away
-        for r in range(1, per):
-            total = total + pltpu.roll(away, ROWS - r, 0)
-        for at, d in enumerate(offsets):
-            out[ROUNDS + d, i : i + 1, :] = total[at * per : at * per + 1, :block]
+            arrived(back.at[d - 1, source], back_sem.at[d - 1, source])
+        total = channel_sum([back[d - 1, source] for source in range(n_grp)])
+        out[ROUNDS + d] = total[:, :block]
     for copy in copies:
         copy.wait_send()
 
@@ -287,7 +294,9 @@
     chunks = pix // LANES
     rows = per * chan * chunks
     block = per * n_grp
-    assert block % ROWS == 0 and per * (SPAN - 1) == ROWS
+    assert block % ROWS == 0 and ROWS % (per * ROUNDS) == 0
+    sources = ROWS // per
+    assert n_grp % (sources // ROUNDS) == 0
     maps = per * LAYERS * chunks
     window = pl.pallas_call(
         functools.partial(kernel, n_blk, n_grp),
@@ -297,18 +306,21 @@
         scratch_shapes=[
             pltpu.VMEM((chan, per, pix), jnp.bfloat16),
             pltpu.VMEM((chunks * ROWS, LANES), jnp.float32),
-            pltpu.VMEM((SPAN, n_grp, rows, LANES), jnp.bfloat16),
+            pltpu.VMEM((ROUNDS + 1, n_grp, rows, LANES), jnp.bfloat16),
             pltpu.VMEM((rows, ROWS, LANES), jnp.float32),
             pltpu.VMEM((rows, LANES), jnp.float32),
             pltpu.VMEM((maps, ROWS, LANES), jnp.float32),
             pltpu.VMEM((maps, ROWS, LANES), jnp.float32),
-            pltpu.VMEM((2, ROWS * chan * chunks, LANES), jnp.float32),
-            pltpu.VMEM((per, block // ROWS + n_grp, ROWS, LANES), jnp.float32),
+            pltpu.VMEM((1, ROWS * chan * chunks, LANES), jnp.float32),
+            pltpu.VMEM((ROUNDS * n_grp, per, LANES), jnp.float32),
+            pltpu.VMEM((ROUNDS, n_grp, per, LANES), jnp.float32),
             pltpu.SemaphoreType.DMA,
             pltpu.SemaphoreType.DMA((n_grp,)),
             pltpu.SemaphoreType.DMA((n_grp,)),
-            pltpu.SemaphoreType.DMA((n_grp, SPAN - 1)),
-            pltpu.SemaphoreType.DMA((SPAN, n_grp)),
+            pltpu.SemaphoreType.DMA((n_grp, ROUNDS)),
+            pltpu.SemaphoreType.DMA((ROUNDS, n_grp)),
+            pltpu.SemaphoreType.DMA((ROUNDS * n_grp,)),
+            pltpu.SemaphoreType.DMA((ROUNDS, n_grp)),
         ],
         compiler_params=pltpu.CompilerParams(
             collective_id=0, has_side_effects=True, vmem_limit_bytes=32 * 1024 * 1024

time: 15.2 us -> 18 us (1.18)
  Pallas kernels: 13.7 us -> 16.5 us
    pallas_call x1, Pallas kernels: 13.7 us -> 16.5 us  [per_device(): pl.pallas_call(functools.partial(kernel, n_blk, n_grp), out_shape=jax.Sha...]
where the time goes in v4:
time: 18 us; the launch traced here: 17.8 us
  Pallas kernels  16.5 us (92%)
  local copies, waits for them, and re-layouts  1.3 us (7%)
    pallas_call x1, Pallas kernels, per_device(): pl.pallas_call(functools.partial(kernel, n_blk, n_grp), out_shape=jax.Sha...  16.5 us
    unnamed x3, local copies, waits for them, and re-layouts  1.3 us

profile of v4, /device:TPU:0, one launch (start us, length us, event | category | flops | bytes accessed | tf_op | source)
XLA Modules:
  0.0 17.8 jit_solution(14180337165203633010)
XLA Ops:
  0.0 0.0 copy-start
  0.0 0.7 %copy-done = bf16[2,3,1024]{2,0,1:T(2,128)(2,1)S(1)} copy-done((bf16[2,3,1024]{2,0,1:T(2,128)(2,1)S(1)}, bf16[2,3,1024]{2,0,1:T(2,128)(2,1)}, u32[]{:S(2)}) %copy-start) | copy-done | bytes 12312
  0.7 16.5 %shard_map.17 = f32[5,2,8]{2,1,0:T(2,128)S(1)} custom-call(bf16[3,2,1024]{2,1,0:T(2,128)(2,1)S(1)} %bitcast.3), custom_call_target="tpu_custom_call" | custom-call | tf_op jit(solution)/shard_map/pallas_call | solution.py:301
  17.2 0.6 %copy.3 = f32[2,5,8]{2,0,1:T(2,128)} copy(f32[2,5,8]{2,0,1:T(2,128)S(1)} %bitcast.2) | data formatting | bytes 640
Async XLA Ops:
  0.0 0.7 %copy-start = (bf16[2,3,1024]{2,0,1:T(2,128)(2,1)S(1)}, bf16[2,3,1024]{2,0,1:T(2,128)(2,1)}, u32[]{:S(2)}) copy-start(bf16[2,3,1024]{2,0,1:T(2,128)(2,1)} %param.1) | copy-start | bytes 36868

commit v5 on v3

--- a/solution.py
+++ b/solution.py
@@ -78,7 +78,7 @@
 
 def kernel(
     n_blk, n_grp, images, out, raw, turn, got, own, flat, root, inv, wide, res,
-    raw_sem, grp_send, grp_recv, blk_send, blk_recv,
+    raw_sem, send, recv,
 ):
     b, z = lax.axis_index("blk"), lax.axis_index("grp")
     chan, per, pix = images.shape
@@ -92,14 +92,13 @@
     load = pltpu.make_async_copy(images, raw, raw_sem)
     load.start()
     barrier = pltpu.get_barrier_semaphore()
-    for dz in range(1, n_grp):
-        pl.semaphore_signal(
-            barrier, inc=1, device_id={"grp": lax.rem(z + dz, n_grp)}, device_id_type=MESH
-        )
-    for d in offsets:
-        pl.semaphore_signal(
-            barrier, inc=1, device_id={"blk": lax.rem(b + d + n_blk, n_blk)}, device_id_type=MESH
-        )
+    def partner(dz, d):
+        return {"blk": lax.rem(b + d + n_blk, n_blk), "grp": lax.rem(z + dz, n_grp)}
+
+    partners = [(0, d) for d in offsets]
+    partners += [(dz, d) for dz in range(1, n_grp) for d in [0] + offsets]
+    for dz, d in partners:
+        pl.semaphore_signal(barrier, inc=1, device_id=partner(dz, d), device_id_type=MESH)
     load.wait()
 
     data = raw[...].astype(jnp.float32)
@@ -122,35 +121,20 @@
         flat[pl.ds(k, per * chan, stride=chunks), :] = row[: per * chan]
     got[ROUNDS, z] = flat[...].astype(jnp.bfloat16)
 
-    pl.semaphore_wait(barrier, n_grp - 1 + len(offsets))
+    pl.semaphore_wait(barrier, len(partners))
 
     copies = []
-    for dz in range(1, n_grp):
+    for dz, d in partners:
         copy = pltpu.make_async_remote_copy(
             src_ref=got.at[ROUNDS, z],
-            dst_ref=got.at[ROUNDS, z],
-            send_sem=grp_send.at[dz],
-            recv_sem=grp_recv.at[z],
-            device_id={"grp": lax.rem(z + dz, n_grp)},
+            dst_ref=got.at[ROUNDS - d, z],
+            send_sem=send.at[dz, ROUNDS + d],
+            recv_sem=recv.at[ROUNDS - d, z],
+            device_id=partner(dz, d),
             device_id_type=MESH,
         )
         copy.start()
         copies.append(copy)
-
-    def pass_on(source, order):
-        for at, d in enumerate(offsets):
-            copy = pltpu.make_async_remote_copy(
-                src_ref=got.at[ROUNDS, source],
-                dst_ref=got.at[ROUNDS + d, source],
-                send_sem=blk_send.at[order, at],
-                recv_sem=blk_recv.at[ROUNDS + d, source],
-                device_id={"blk": lax.rem(b - d + n_blk, n_blk)},
-                device_id_type=MESH,
-            )
-            copy.start()
-            copies.append(copy)
-
-    pass_on(z, 0)
 
     masks = lane_masks()
     current = []
@@ -175,20 +159,15 @@
                 root[at] = roots[k]
                 inv[at] = inverses[k]
 
-    def arrived(k, source, sem):
+    def arrived(k, source):
         pltpu.make_async_remote_copy(
             src_ref=got.at[k, source],
             dst_ref=got.at[k, source],
-            send_sem=grp_send.at[0],
-            recv_sem=sem,
+            send_sem=send.at[0, 0],
+            recv_sem=recv.at[k, source],
             device_id={"grp": z},
             device_id_type=MESH,
         ).wait_recv()
-
-    for dz in range(1, n_grp):
-        source = lax.rem(z + dz, n_grp)
-        arrived(ROUNDS, source, grp_recv.at[source])
-        pass_on(source, dz)
 
     def work(members):
         maps = []
@@ -239,7 +218,12 @@
         @pl.when(home == 0)
         def _():
             for d in offsets:
-                arrived(ROUNDS + d, source, blk_recv.at[ROUNDS + d, source])
+                arrived(ROUNDS + d, source)
+
+        @pl.when(t == 1)
+        def _():
+            for dz in range(1, n_grp):
+                arrived(ROUNDS, lax.rem(z + dz, n_grp))
 
         unit = home * (t - 1)
         places = [
@@ -305,9 +289,7 @@
             pltpu.VMEM((2, ROWS * chan * chunks, LANES), jnp.float32),
             pltpu.VMEM((per, block // ROWS + n_grp, ROWS, LANES), jnp.float32),
             pltpu.SemaphoreType.DMA,
-            pltpu.SemaphoreType.DMA((n_grp,)),
-            pltpu.SemaphoreType.DMA((n_grp,)),
-            pltpu.SemaphoreType.DMA((n_grp, SPAN - 1)),
+            pltpu.SemaphoreType.DMA((n_grp, SPAN)),
             pltpu.SemaphoreType.DMA((SPAN, n_grp)),
         ],
         compiler_params=pltpu.CompilerParams(

time: 15.2 us -> 15.6 us (1.026)
  Pallas kernels: 13.7 us -> 14.1 us
    pallas_call x1, Pallas kernels: 13.7 us -> 14.1 us  [per_device(): pl.pallas_call(functools.partial(kernel, n_blk, n_grp), out_shape=jax.Sha...]
where the time goes in v5:
time: 15.6 us; the launch traced here: 15.4 us
  Pallas kernels  14.1 us (90%)
  local copies, waits for them, and re-layouts  1.3 us (8%)
    pallas_call x1, Pallas kernels, per_device(): pl.pallas_call(functools.partial(kernel, n_blk, n_grp), out_shape=jax.Sha...  14.1 us
    unnamed x3, local copies, waits for them, and re-layouts  1.3 us

profile of v5, /device:TPU:0, one launch (start us, length us, event | category | flops | bytes accessed | tf_op | source)
XLA Modules:
  0.0 15.4 jit_solution(5004232696055259526)
XLA Ops:
  0.0 0.0 copy-start
  0.0 0.7 %copy-done = bf16[2,3,1024]{2,0,1:T(2,128)(2,1)S(1)} copy-done((bf16[2,3,1024]{2,0,1:T(2,128)(2,1)S(1)}, bf16[2,3,1024]{2,0,1:T(2,128)(2,1)}, u32[]{:S(2)}) %copy-start) | copy-done | bytes 12312
  0.7 14.1 %shard_map.17 = f32[5,2,8]{2,1,0:T(2,128)S(1)} custom-call(bf16[3,2,1024]{2,1,0:T(2,128)(2,1)S(1)} %bitcast.3), custom_call_target="tpu_custom_call" | custom-call | tf_op jit(solution)/shard_map/pallas_call | solution.py:276
  14.8 0.6 %copy.3 = f32[2,5,8]{2,0,1:T(2,128)} copy(f32[2,5,8]{2,0,1:T(2,128)S(1)} %bitcast.2) | data formatting | bytes 640
Async XLA Ops:
  0.0 0.7 %copy-start = (bf16[2,3,1024]{2,0,1:T(2,128)(2,1)S(1)}, bf16[2,3,1024]{2,0,1:T(2,128)(2,1)}, u32[]{:S(2)}) copy-start(bf16[2,3,1024]{2,0,1:T(2,128)(2,1)} %param.1) | copy-start | bytes 36868

commit v6 on v3

--- a/solution.py
+++ b/solution.py
@@ -311,7 +311,7 @@
             pltpu.SemaphoreType.DMA((SPAN, n_grp)),
         ],
         compiler_params=pltpu.CompilerParams(
-            collective_id=0, has_side_effects=True, vmem_limit_bytes=32 * 1024 * 1024
+            collective_id=0, has_side_effects=True, vmem_limit_bytes=60 * 1024 * 1024
         ),
     )(jnp.transpose(images, (1, 0, 2)))
     return jnp.transpose(window, (1, 0, 2))

time: 15.2 us -> 15.8 us (1.039)
  Pallas kernels: 13.7 us -> 14.3 us
    pallas_call x1, Pallas kernels: 13.7 us -> 14.3 us  [per_device(): pl.pallas_call(functools.partial(kernel, n_blk, n_grp), out_shape=jax.Sha...]
    unnamed x3 -> x1, local copies, waits for them, and re-layouts: 1.3 us -> 1.28 us
where the time goes in v6:
time: 15.8 us; the launch traced here: 15.6 us
  Pallas kernels  14.3 us (91%)
  local copies, waits for them, and re-layouts  1.28 us (8%)
    pallas_call x1, Pallas kernels, per_device(): pl.pallas_call(functools.partial(kernel, n_blk, n_grp), out_shape=jax.Sha...  14.3 us
    unnamed x1, local copies, waits for them, and re-layouts  1.28 us

profile of v6, /device:TPU:0, one launch (start us, length us, event | category | flops | bytes accessed | tf_op | source)
XLA Modules:
  0.0 15.6 jit_solution(3002006624949886752)
XLA Ops:
  0.0 14.3 %shard_map.17 = f32[5,2,8]{2,1,0:T(2,128)} custom-call(bf16[3,2,1024]{2,1,0:T(2,128)(2,1)} %bitcast.3), custom_call_target="tpu_custom_call" | custom-call | tf_op jit(solution)/shard_map/pallas_call | solution.py:292
  14.3 1.3 %copy.3 = f32[2,5,8]{2,0,1:T(2,128)} copy(f32[2,5,8]{2,0,1:T(2,128)} %bitcast.2) | data formatting | bytes 640

commit v7 on v5

--- a/solution.py
+++ b/solution.py
@@ -92,13 +92,23 @@
     load = pltpu.make_async_copy(images, raw, raw_sem)
     load.start()
     barrier = pltpu.get_barrier_semaphore()
-    def partner(dz, d):
-        return {"blk": lax.rem(b + d + n_blk, n_blk), "grp": lax.rem(z + dz, n_grp)}
-
-    partners = [(0, d) for d in offsets]
-    partners += [(dz, d) for dz in range(1, n_grp) for d in [0] + offsets]
-    for dz, d in partners:
-        pl.semaphore_signal(barrier, inc=1, device_id=partner(dz, d), device_id_type=MESH)
+    def source_of(order):
+        if isinstance(order, int) and order == 0:
+            return z
+        mate = z + 1 - 2 * lax.rem(z, 2)
+        far = lax.rem(z // 2 * 2 + order, n_grp)
+        if isinstance(order, int):
+            return mate if order == 1 else far
+        return jnp.where(order == 0, z, jnp.where(order == 1, mate, far))
+
+    partners = [(0, d) for d in offsets] + [(1, d) for d in [0] + offsets]
+    partners += [(order, 0) for order in range(2, n_grp)]
+    partners = [
+        (order, d, {"blk": lax.rem(b + d + n_blk, n_blk), "grp": source_of(order)})
+        for order, d in partners
+    ]
+    for order, d, device in partners:
+        pl.semaphore_signal(barrier, inc=1, device_id=device, device_id_type=MESH)
     load.wait()
 
     data = raw[...].astype(jnp.float32)
@@ -124,17 +134,21 @@
     pl.semaphore_wait(barrier, len(partners))
 
     copies = []
-    for dz, d in partners:
+
+    def give(order, source, d, device):
         copy = pltpu.make_async_remote_copy(
-            src_ref=got.at[ROUNDS, z],
-            dst_ref=got.at[ROUNDS - d, z],
-            send_sem=send.at[dz, ROUNDS + d],
-            recv_sem=recv.at[ROUNDS - d, z],
-            device_id=partner(dz, d),
+            src_ref=got.at[ROUNDS, source],
+            dst_ref=got.at[ROUNDS - d, source],
+            send_sem=send.at[order, ROUNDS + d],
+            recv_sem=recv.at[ROUNDS - d, source],
+            device_id=device,
             device_id_type=MESH,
         )
         copy.start()
         copies.append(copy)
+
+    for order, d, device in sorted(partners, key=lambda p: p[0] < 2):
+        give(order, z, d, device)
 
     masks = lane_masks()
     current = []
@@ -163,11 +177,18 @@
         pltpu.make_async_remote_copy(
             src_ref=got.at[k, source],
             dst_ref=got.at[k, source],
-            send_sem=send.at[0, 0],
+            send_sem=send.at[0, ROUNDS],
             recv_sem=recv.at[k, source],
             device_id={"grp": z},
             device_id_type=MESH,
         ).wait_recv()
+
+    for order in range(2, n_grp):
+        source = source_of(order)
+        arrived(ROUNDS, source)
+        for d in offsets:
+            give(order, source, d, {"blk": lax.rem(b + d + n_blk, n_blk)})
+    arrived(ROUNDS, source_of(1))
 
     def work(members):
         maps = []
@@ -213,17 +234,12 @@
         home = jnp.int32((t >= 1) & (t <= units))
         away = 1 - home
         order = jnp.where(t > units, t - units, 0)
-        source = lax.rem(z + order, n_grp)
+        source = source_of(order)
 
         @pl.when(home == 0)
         def _():
             for d in offsets:
                 arrived(ROUNDS + d, source)
-
-        @pl.when(t == 1)
-        def _():
-            for dz in range(1, n_grp):
-                arrived(ROUNDS, lax.rem(z + dz, n_grp))
 
         unit = home * (t - 1)
         places = [
@@ -271,7 +287,7 @@
     chunks = pix // LANES
     rows = per * chan * chunks
     block = per * n_grp
-    assert block % ROWS == 0 and per * (SPAN - 1) == ROWS
+    assert n_grp % 2 == 0 and block % ROWS == 0 and per * (SPAN - 1) == ROWS
     maps = per * LAYERS * chunks
     window = pl.pallas_call(
         functools.partial(kernel, n_blk, n_grp),

time: 15.6 us -> 15.1 us (0.968)
  Pallas kernels: 14.1 us -> 13.6 us
    pallas_call x1, Pallas kernels: 14.1 us -> 13.6 us  [per_device(): pl.pallas_call(functools.partial(kernel, n_blk, n_grp), out_shape=jax.Sha...]
where the time goes in v7:
time: 15.1 us; the launch traced here: 14.9 us
  Pallas kernels  13.6 us (90%)
  local copies, waits for them, and re-layouts  1.3 us (9%)
    pallas_call x1, Pallas kernels, per_device(): pl.pallas_call(functools.partial(kernel, n_blk, n_grp), out_shape=jax.Sha...  13.6 us
    unnamed x3, local copies, waits for them, and re-layouts  1.3 us

profile of v7, /device:TPU:0, one launch (start us, length us, event | category | flops | bytes accessed | tf_op | source)
XLA Modules:
  0.0 14.9 jit_solution(12772957582744191990)
XLA Ops:
  0.0 0.0 copy-start
  0.0 0.7 %copy-done = bf16[2,3,1024]{2,0,1:T(2,128)(2,1)S(1)} copy-done((bf16[2,3,1024]{2,0,1:T(2,128)(2,1)S(1)}, bf16[2,3,1024]{2,0,1:T(2,128)(2,1)}, u32[]{:S(2)}) %copy-start) | copy-done | bytes 12312
  0.7 13.6 %shard_map.17 = f32[5,2,8]{2,1,0:T(2,128)S(1)} custom-call(bf16[3,2,1024]{2,1,0:T(2,128)(2,1)S(1)} %bitcast.3), custom_call_target="tpu_custom_call" | custom-call | tf_op jit(solution)/shard_map/pallas_call | solution.py:292
  14.3 0.6 %copy.3 = f32[2,5,8]{2,0,1:T(2,128)} copy(f32[2,5,8]{2,0,1:T(2,128)S(1)} %bitcast.2) | data formatting | bytes 640
Async XLA Ops:
  0.0 0.7 %copy-start = (bf16[2,3,1024]{2,0,1:T(2,128)(2,1)S(1)}, bf16[2,3,1024]{2,0,1:T(2,128)(2,1)}, u32[]{:S(2)}) copy-start(bf16[2,3,1024]{2,0,1:T(2,128)(2,1)} %param.1) | copy-start | bytes 36868

commit v8 on v3

--- a/solution.py
+++ b/solution.py
@@ -77,8 +77,8 @@
 
 
 def kernel(
-    n_blk, n_grp, images, out, raw, turn, got, own, flat, root, inv, wide, res,
-    raw_sem, grp_send, grp_recv, blk_send, blk_recv,
+    n_blk, n_grp, images, out, turn, got, own, flat, root, inv, wide, res,
+    grp_send, grp_recv, blk_send, blk_recv,
 ):
     b, z = lax.axis_index("blk"), lax.axis_index("grp")
     chan, per, pix = images.shape
@@ -89,8 +89,6 @@
     sources = ROWS // per
     offsets = [d for d in range(-ROUNDS, ROUNDS + 1) if d]
 
-    load = pltpu.make_async_copy(images, raw, raw_sem)
-    load.start()
     barrier = pltpu.get_barrier_semaphore()
     for dz in range(1, n_grp):
         pl.semaphore_signal(
@@ -100,9 +98,8 @@
         pl.semaphore_signal(
             barrier, inc=1, device_id={"blk": lax.rem(b + d + n_blk, n_blk)}, device_id_type=MESH
         )
-    load.wait()
-
-    data = raw[...].astype(jnp.float32)
+
+    data = images[...].astype(jnp.float32)
     for k in range(chunks):
         for c in range(chan):
             turn[pl.ds(k * ROWS + c, per, stride=chan), :] = data[
@@ -120,37 +117,39 @@
             part = pltpu.roll(part, shift, 1) if shift else part
             row = part if row is None else jnp.where(lane >= g * SIDE, part, row)
         flat[pl.ds(k, per * chan, stride=chunks), :] = row[: per * chan]
-    got[ROUNDS, z] = flat[...].astype(jnp.bfloat16)
+    got[ROUNDS, 0] = flat[...].astype(jnp.bfloat16)
 
     pl.semaphore_wait(barrier, n_grp - 1 + len(offsets))
 
     copies = []
     for dz in range(1, n_grp):
         copy = pltpu.make_async_remote_copy(
-            src_ref=got.at[ROUNDS, z],
-            dst_ref=got.at[ROUNDS, z],
+            src_ref=got.at[ROUNDS, 0],
+            dst_ref=got.at[ROUNDS, n_grp - dz],
             send_sem=grp_send.at[dz],
-            recv_sem=grp_recv.at[z],
+            recv_sem=grp_recv.at[n_grp - dz],
             device_id={"grp": lax.rem(z + dz, n_grp)},
             device_id_type=MESH,
         )
         copy.start()
         copies.append(copy)
 
-    def pass_on(source, order):
+    stages = [pl.ds(0, 1), pl.ds(1, n_grp - 1)]
+
+    def pass_on(stage):
         for at, d in enumerate(offsets):
             copy = pltpu.make_async_remote_copy(
-                src_ref=got.at[ROUNDS, source],
-                dst_ref=got.at[ROUNDS + d, source],
-                send_sem=blk_send.at[order, at],
-                recv_sem=blk_recv.at[ROUNDS + d, source],
+                src_ref=got.at[ROUNDS, stages[stage]],
+                dst_ref=got.at[ROUNDS + d, stages[stage]],
+                send_sem=blk_send.at[stage, at],
+                recv_sem=blk_recv.at[stage, at],
                 device_id={"blk": lax.rem(b - d + n_blk, n_blk)},
                 device_id_type=MESH,
             )
             copy.start()
             copies.append(copy)
 
-    pass_on(z, 0)
+    pass_on(0)
 
     masks = lane_masks()
     current = []
@@ -175,10 +174,10 @@
                 root[at] = roots[k]
                 inv[at] = inverses[k]
 
-    def arrived(k, source, sem):
+    def arrived(ref, sem):
         pltpu.make_async_remote_copy(
-            src_ref=got.at[k, source],
-            dst_ref=got.at[k, source],
+            src_ref=ref,
+            dst_ref=ref,
             send_sem=grp_send.at[0],
             recv_sem=sem,
             device_id={"grp": z},
@@ -186,9 +185,8 @@
         ).wait_recv()
 
     for dz in range(1, n_grp):
-        source = lax.rem(z + dz, n_grp)
-        arrived(ROUNDS, source, grp_recv.at[source])
-        pass_on(source, dz)
+        arrived(got.at[ROUNDS, dz], grp_recv.at[dz])
+    pass_on(1)
 
     def work(members):
         maps = []
@@ -236,14 +234,19 @@
         order = jnp.where(t > units, t - units, 0)
         source = lax.rem(z + order, n_grp)
 
-        @pl.when(home == 0)
-        def _():
-            for d in offsets:
-                arrived(ROUNDS + d, source, blk_recv.at[ROUNDS + d, source])
+        for stage, when in enumerate((0, units + 1)):
+
+            @pl.when(t == when)
+            def _():
+                for at, d in enumerate(offsets):
+                    arrived(got.at[ROUNDS + d, stages[stage]], blk_recv.at[stage, at])
 
         unit = home * (t - 1)
         places = [
-            (ROUNDS + away * d, away * source + home * (unit * sources + s))
+            (
+                ROUNDS + away * d,
+                away * order + home * lax.rem(unit * sources + s - z + n_grp, n_grp),
+            )
             for s, d in enumerate(offsets)
         ]
         return places, home * unit + away * (units + source)
@@ -292,10 +295,9 @@
     window = pl.pallas_call(
         functools.partial(kernel, n_blk, n_grp),
         out_shape=jax.ShapeDtypeStruct((SPAN, per, block), jnp.float32),
-        in_specs=[pl.BlockSpec(memory_space=pltpu.HBM)],
+        in_specs=[pl.BlockSpec(memory_space=pltpu.VMEM)],
         out_specs=pl.BlockSpec(memory_space=pltpu.VMEM),
         scratch_shapes=[
-            pltpu.VMEM((chan, per, pix), jnp.bfloat16),
             pltpu.VMEM((chunks * ROWS, LANES), jnp.float32),
             pltpu.VMEM((SPAN, n_grp, rows, LANES), jnp.bfloat16),
             pltpu.VMEM((rows, ROWS, LANES), jnp.float32),
@@ -304,11 +306,10 @@
             pltpu.VMEM((maps, ROWS, LANES), jnp.float32),
             pltpu.VMEM((2, ROWS * chan * chunks, LANES), jnp.float32),
             pltpu.VMEM((per, block // ROWS + n_grp, ROWS, LANES), jnp.float32),
-            pltpu.SemaphoreType.DMA,
             pltpu.SemaphoreType.DMA((n_grp,)),
             pltpu.SemaphoreType.DMA((n_grp,)),
-            pltpu.SemaphoreType.DMA((n_grp, SPAN - 1)),
-            pltpu.SemaphoreType.DMA((SPAN, n_grp)),
+            pltpu.SemaphoreType.DMA((2, SPAN - 1)),
+            pltpu.SemaphoreType.DMA((2, SPAN - 1)),
         ],
         compiler_params=pltpu.CompilerParams(
             collective_id=0, has_side_effects=True, vmem_limit_bytes=32 * 1024 * 1024

time: 15.2 us -> 15.5 us (1.020)
  Pallas kernels: 13.7 us -> 14 us
    pallas_call x1, Pallas kernels: 13.7 us -> 14 us  [per_device(): pl.pallas_call(functools.partial(kernel, n_blk, n_grp), out_shape=jax.Sha...]
where the time goes in v8:
time: 15.5 us; the launch traced here: 15.3 us
  Pallas kernels  14 us (90%)
  local copies, waits for them, and re-layouts  1.3 us (8%)
    pallas_call x1, Pallas kernels, per_device(): pl.pallas_call(functools.partial(kernel, n_blk, n_grp), out_shape=jax.Sha...  14 us
    unnamed x3, local copies, waits for them, and re-layouts  1.3 us

profile of v8, /device:TPU:0, one launch (start us, length us, event | category | flops | bytes accessed | tf_op | source)
XLA Modules:
  0.0 15.3 jit_solution(12450208399618137283)
XLA Ops:
  0.0 0.0 copy-start
  0.0 0.7 %copy-done = bf16[2,3,1024]{2,0,1:T(2,128)(2,1)S(1)} copy-done((bf16[2,3,1024]{2,0,1:T(2,128)(2,1)S(1)}, bf16[2,3,1024]{2,0,1:T(2,128)(2,1)}, u32[]{:S(2)}) %copy-start) | copy-done | bytes 12312
  0.7 14.0 %shard_map.17 = f32[5,2,8]{2,1,0:T(2,128)S(1)} custom-call(bf16[3,2,1024]{2,1,0:T(2,128)(2,1)S(1)} %bitcast.3), custom_call_target="tpu_custom_call" | custom-call | tf_op jit(solution)/shard_map/pallas_call | solution.py:295
  14.7 0.6 %copy.3 = f32[2,5,8]{2,0,1:T(2,128)} copy(f32[2,5,8]{2,0,1:T(2,128)S(1)} %bitcast.2) | data formatting | bytes 640
Async XLA Ops:
  0.0 0.7 %copy-start = (bf16[2,3,1024]{2,0,1:T(2,128)(2,1)S(1)}, bf16[2,3,1024]{2,0,1:T(2,128)(2,1)}, u32[]{:S(2)}) copy-start(bf16[2,3,1024]{2,0,1:T(2,128)(2,1)} %param.1) | copy-start | bytes 36868

commit v9 on v7

--- a/solution.py
+++ b/solution.py
@@ -77,8 +77,8 @@
 
 
 def kernel(
-    n_blk, n_grp, images, out, raw, turn, got, own, flat, root, inv, wide, res,
-    raw_sem, send, recv,
+    n_blk, n_grp, images, out, turn, got, own, flat, root, inv, wide, res,
+    send, recv,
 ):
     b, z = lax.axis_index("blk"), lax.axis_index("grp")
     chan, per, pix = images.shape
@@ -89,8 +89,6 @@
     sources = ROWS // per
     offsets = [d for d in range(-ROUNDS, ROUNDS + 1) if d]
 
-    load = pltpu.make_async_copy(images, raw, raw_sem)
-    load.start()
     barrier = pltpu.get_barrier_semaphore()
     def source_of(order):
         if isinstance(order, int) and order == 0:
@@ -109,9 +107,8 @@
     ]
     for order, d, device in partners:
         pl.semaphore_signal(barrier, inc=1, device_id=device, device_id_type=MESH)
-    load.wait()
-
-    data = raw[...].astype(jnp.float32)
+
+    data = images[...].astype(jnp.float32)
     for k in range(chunks):
         for c in range(chan):
             turn[pl.ds(k * ROWS + c, per, stride=chan), :] = data[
@@ -251,12 +248,10 @@
     total_units = units + n_grp
 
     def step(t, carry):
-        work([member(2 * t), member(2 * t + 1)])
+        work([member(t)])
         return carry
 
-    lax.fori_loop(0, total_units // 2, step, 0)
-    if total_units % 2:
-        work([member(jnp.int32(total_units - 1))])
+    lax.fori_loop(0, total_units, step, 0)
 
     row = lax.broadcasted_iota(jnp.int32, (ROWS, LANES), 0)
     lane = lax.broadcasted_iota(jnp.int32, (ROWS, LANES), 1)
@@ -292,19 +287,17 @@
     window = pl.pallas_call(
         functools.partial(kernel, n_blk, n_grp),
         out_shape=jax.ShapeDtypeStruct((SPAN, per, block), jnp.float32),
-        in_specs=[pl.BlockSpec(memory_space=pltpu.HBM)],
+        in_specs=[pl.BlockSpec(memory_space=pltpu.VMEM)],
         out_specs=pl.BlockSpec(memory_space=pltpu.VMEM),
         scratch_shapes=[
-            pltpu.VMEM((chan, per, pix), jnp.bfloat16),
             pltpu.VMEM((chunks * ROWS, LANES), jnp.float32),
             pltpu.VMEM((SPAN, n_grp, rows, LANES), jnp.bfloat16),
             pltpu.VMEM((rows, ROWS, LANES), jnp.float32),
             pltpu.VMEM((rows, LANES), jnp.float32),
             pltpu.VMEM((maps, ROWS, LANES), jnp.float32),
             pltpu.VMEM((maps, ROWS, LANES), jnp.float32),
-            pltpu.VMEM((2, ROWS * chan * chunks, LANES), jnp.float32),
+            pltpu.VMEM((1, ROWS * chan * chunks, LANES), jnp.float32),
             pltpu.VMEM((per, block // ROWS + n_grp, ROWS, LANES), jnp.float32),
-            pltpu.SemaphoreType.DMA,
             pltpu.SemaphoreType.DMA((n_grp, SPAN)),
             pltpu.SemaphoreType.DMA((SPAN, n_grp)),
         ],

time: 15.1 us -> 15 us (level)
  Pallas kernels: 13.6 us -> 13.4 us
where the time goes in v9:
time: 15 us; the launch traced here: 14.8 us
  Pallas kernels  13.4 us (89%)
  local copies, waits for them, and re-layouts  1.3 us (9%)
    pallas_call x1, Pallas kernels, per_device(): pl.pallas_call(functools.partial(kernel, n_blk, n_grp), out_shape=jax.Sha...  13.4 us
    unnamed x3, local copies, waits for them, and re-layouts  1.3 us

profile of v9, /device:TPU:0, one launch (start us, length us, event | category | flops | bytes accessed | tf_op | source)
XLA Modules:
  0.0 14.8 jit_solution(11366113543879100202)
XLA Ops:
  0.0 0.0 copy-start
  0.0 0.7 %copy-done = bf16[2,3,1024]{2,0,1:T(2,128)(2,1)S(1)} copy-done((bf16[2,3,1024]{2,0,1:T(2,128)(2,1)S(1)}, bf16[2,3,1024]{2,0,1:T(2,128)(2,1)}, u32[]{:S(2)}) %copy-start) | copy-done | bytes 12312
  0.7 13.4 %shard_map.17 = f32[5,2,8]{2,1,0:T(2,128)S(1)} custom-call(bf16[3,2,1024]{2,1,0:T(2,128)(2,1)S(1)} %bitcast.3), custom_call_target="tpu_custom_call" | custom-call | tf_op jit(solution)/shard_map/pallas_call | solution.py:287
  14.2 0.6 %copy.3 = f32[2,5,8]{2,0,1:T(2,128)} copy(f32[2,5,8]{2,0,1:T(2,128)S(1)} %bitcast.2) | data formatting | bytes 640
Async XLA Ops:
  0.0 0.7 %copy-start = (bf16[2,3,1024]{2,0,1:T(2,128)(2,1)S(1)}, bf16[2,3,1024]{2,0,1:T(2,128)(2,1)}, u32[]{:S(2)}) copy-start(bf16[2,3,1024]{2,0,1:T(2,128)(2,1)} %param.1) | copy-start | bytes 36868

commit v10 on v9

--- a/solution.py
+++ b/solution.py
@@ -18,12 +18,11 @@
 MESH = pl.DeviceIdType.MESH
 
 ARC = (
-    0.3183098449892848,
-    -0.02253203775558662,
-    0.005946535585369838,
-    -0.002275705294168609,
-    0.0008254564785290766,
-    -0.00016869743862866002,
+    0.3183095237082206,
+    -0.02251588221055572,
+    0.005816643278465437,
+    -0.0019102241839555419,
+    0.00040573672732109817,
 )
 
 
@@ -57,8 +56,12 @@
     return total
 
 
-def affine(groups, factor):
-    return [[x * factor + BIAS for x in maps] for maps in groups]
+def map_scale(channels, layer):
+    return float(channels * 9 ** (layer + 1))
+
+
+def biased(groups, scale):
+    return [[x + BIAS * scale for x in maps] for maps in groups]
 
 
 def roots_of(maps):
@@ -161,8 +164,7 @@
             squares.append(channel_sum(parts))
         current.append(squares)
     for layer in range(LAYERS):
-        factor = 1.0 / 9 if layer else 1.0 / (9 * chan)
-        current = affine(stencil_sum(current, masks), factor)
+        current = biased(stencil_sum(current, masks), map_scale(chan, layer))
         for i in range(per):
             roots, inverses = roots_of(current[i])
             for k in range(chunks):
@@ -212,8 +214,7 @@
                     ]
                 )
         for layer in range(LAYERS):
-            factor = 1.0 / 9 if layer else 1.0 / (9 * chan)
-            maps = affine(stencil_sum(maps, masks), factor)
+            maps = biased(stencil_sum(maps, masks), map_scale(chan, layer))
             for m in range(len(members)):
                 roots, inverses = roots_of(maps[m * (per + 1)])
                 for i in range(per):
@@ -257,7 +258,8 @@
     lane = lax.broadcasted_iota(jnp.int32, (ROWS, LANES), 1)
     for i in range(per):
         sums = [
-            jnp.sum(res[i, slot], axis=1, keepdims=True) * (1.0 / pix)
+            jnp.sum(res[i, slot], axis=1, keepdims=True)
+            * (1.0 / (pix * map_scale(chan, LAYERS - 1)))
             for slot in range(units + n_grp)
         ]
         home = jnp.zeros((ROWS, LANES), jnp.float32)

time: 15 us -> 15 us (level)
  no operation moved by 1% of the time
where the time goes in v10:
time: 15 us; the launch traced here: 14.7 us
  Pallas kernels  13.4 us (89%)
  local copies, waits for them, and re-layouts  1.3 us (9%)
    pallas_call x1, Pallas kernels, per_device(): pl.pallas_call(functools.partial(kernel, n_blk, n_grp), out_shape=jax.Sha...  13.4 us
    unnamed x3, local copies, waits for them, and re-layouts  1.3 us

profile of v10, /device:TPU:0, one launch (start us, length us, event | category | flops | bytes accessed | tf_op | source)
XLA Modules:
  0.0 14.7 jit_solution(2266426130933613133)
XLA Ops:
  0.0 0.0 copy-start
  0.0 0.7 %copy-done = bf16[2,3,1024]{2,0,1:T(2,128)(2,1)S(1)} copy-done((bf16[2,3,1024]{2,0,1:T(2,128)(2,1)S(1)}, bf16[2,3,1024]{2,0,1:T(2,128)(2,1)}, u32[]{:S(2)}) %copy-start) | copy-done | bytes 12312
  0.7 13.4 %shard_map.17 = f32[5,2,8]{2,1,0:T(2,128)S(1)} custom-call(bf16[3,2,1024]{2,1,0:T(2,128)(2,1)S(1)} %bitcast.3), custom_call_target="tpu_custom_call" | custom-call | tf_op jit(solution)/shard_map/pallas_call | solution.py:289
  14.1 0.6 %copy.3 = f32[2,5,8]{2,0,1:T(2,128)} copy(f32[2,5,8]{2,0,1:T(2,128)S(1)} %bitcast.2) | data formatting | bytes 640
Async XLA Ops:
  0.0 0.7 %copy-start = (bf16[2,3,1024]{2,0,1:T(2,128)(2,1)S(1)}, bf16[2,3,1024]{2,0,1:T(2,128)(2,1)}, u32[]{:S(2)}) copy-start(bf16[2,3,1024]{2,0,1:T(2,128)(2,1)} %param.1) | copy-start | bytes 36868

commit v11 on v10

--- a/solution.py
+++ b/solution.py
@@ -252,7 +252,7 @@
         work([member(t)])
         return carry
 
-    lax.fori_loop(0, total_units, step, 0)
+    lax.fori_loop(0, total_units, step, 0, unroll=True)
 
     row = lax.broadcasted_iota(jnp.int32, (ROWS, LANES), 0)
     lane = lax.broadcasted_iota(jnp.int32, (ROWS, LANES), 1)

time: 15 us -> 14.9 us (level)
  no operation moved by 1% of the time
where the time goes in v11:
time: 14.9 us; the launch traced here: 14.7 us
  Pallas kernels  13.4 us (90%)
  local copies, waits for them, and re-layouts  1.3 us (9%)
    pallas_call x1, Pallas kernels, per_device(): pl.pallas_call(functools.partial(kernel, n_blk, n_grp), out_shape=jax.Sha...  13.4 us
    unnamed x3, local copies, waits for them, and re-layouts  1.3 us

profile of v11, /device:TPU:0, one launch (start us, length us, event | category | flops | bytes accessed | tf_op | source)
XLA Modules:
  0.0 14.7 jit_solution(16331882198584794580)
XLA Ops:
  0.0 0.0 copy-start
  0.0 0.7 %copy-done = bf16[2,3,1024]{2,0,1:T(2,128)(2,1)S(1)} copy-done((bf16[2,3,1024]{2,0,1:T(2,128)(2,1)S(1)}, bf16[2,3,1024]{2,0,1:T(2,128)(2,1)}, u32[]{:S(2)}) %copy-start) | copy-done | bytes 12312
  0.7 13.4 %shard_map.17 = f32[5,2,8]{2,1,0:T(2,128)S(1)} custom-call(bf16[3,2,1024]{2,1,0:T(2,128)(2,1)S(1)} %bitcast.3), custom_call_target="tpu_custom_call" | custom-call | tf_op jit(solution)/shard_map/pallas_call | solution.py:289
  14.1 0.6 %copy.3 = f32[2,5,8]{2,0,1:T(2,128)} copy(f32[2,5,8]{2,0,1:T(2,128)S(1)} %bitcast.2) | data formatting | bytes 640
Async XLA Ops:
  0.0 0.7 %copy-start = (bf16[2,3,1024]{2,0,1:T(2,128)(2,1)S(1)}, bf16[2,3,1024]{2,0,1:T(2,128)(2,1)}, u32[]{:S(2)}) copy-start(bf16[2,3,1024]{2,0,1:T(2,128)(2,1)} %param.1) | copy-start | bytes 36868

commit v12 on v11

--- a/solution.py
+++ b/solution.py
@@ -229,7 +229,7 @@
                 res[i, slot] = channel_sum(maps[m * (per + 1) + 1 + i])
 
     def member(t):
-        home = jnp.int32((t >= 1) & (t <= units))
+        home = jnp.int32(t < units)
         away = 1 - home
         order = jnp.where(t > units, t - units, 0)
         source = source_of(order)
@@ -239,7 +239,7 @@
             for d in offsets:
                 arrived(ROUNDS + d, source)
 
-        unit = home * (t - 1)
+        unit = home * t
         places = [
             (ROUNDS + away * d, away * source + home * (unit * sources + s))
             for s, d in enumerate(offsets)

time: 14.9 us -> 14.9 us (level)
  no operation moved by 1% of the time
where the time goes in v12:
time: 14.9 us; the launch traced here: 14.7 us
  Pallas kernels  13.4 us (90%)
  local copies, waits for them, and re-layouts  1.3 us (9%)
    pallas_call x1, Pallas kernels, per_device(): pl.pallas_call(functools.partial(kernel, n_blk, n_grp), out_shape=jax.Sha...  13.4 us
    unnamed x3, local copies, waits for them, and re-layouts  1.3 us

profile of v12, /device:TPU:0, one launch (start us, length us, event | category | flops | bytes accessed | tf_op | source)
XLA Modules:
  0.0 14.7 jit_solution(17266364920951116999)
XLA Ops:
  0.0 0.0 copy-start
  0.0 0.7 %copy-done = bf16[2,3,1024]{2,0,1:T(2,128)(2,1)S(1)} copy-done((bf16[2,3,1024]{2,0,1:T(2,128)(2,1)S(1)}, bf16[2,3,1024]{2,0,1:T(2,128)(2,1)}, u32[]{:S(2)}) %copy-start) | copy-done | bytes 12312
  0.7 13.4 %shard_map.17 = f32[5,2,8]{2,1,0:T(2,128)S(1)} custom-call(bf16[3,2,1024]{2,1,0:T(2,128)(2,1)S(1)} %bitcast.3), custom_call_target="tpu_custom_call" | custom-call | tf_op jit(solution)/shard_map/pallas_call | solution.py:289
  14.1 0.6 %copy.3 = f32[2,5,8]{2,0,1:T(2,128)} copy(f32[2,5,8]{2,0,1:T(2,128)S(1)} %bitcast.2) | data formatting | bytes 640
Async XLA Ops:
  0.0 0.7 %copy-start = (bf16[2,3,1024]{2,0,1:T(2,128)(2,1)S(1)}, bf16[2,3,1024]{2,0,1:T(2,128)(2,1)}, u32[]{:S(2)}) copy-start(bf16[2,3,1024]{2,0,1:T(2,128)(2,1)} %param.1) | copy-start | bytes 36868
